TPU v7x, 32 devices: a whole 2x2x4 slice. The times are simulated.
32 devices in a mesh: tiles: 8 (over z, y), nests: 4 (over x, core).
Axes of the slice: x: 2, y: 2, z: 4, core: 2. Of those that a mesh axis runs over, the one named last changes fastest.
Arguments:
- parent: float32 [512, 1024, 128], P('tiles', 'nests'), may hold values from -6 to 6
- nest_state: float32 [4, 32, 128, 128], P('nests', 'tiles'), may hold values from -6 to 6
- parent_mix: float32 [128, 128], replicated, may hold values from -0.24 to 0.24
- nest_mix: float32 [128, 128], replicated, may hold values from -0.24 to 0.24
- courant: float32 [2, 128], replicated, may hold values from 0.05 to 0.45
- nest_pos: int32 [4, 2], P('nests'), may hold values from 0 to 2882, as said below
Outputs:
- parent_out: float32 [512, 1024, 128], P('tiles', 'nests')
- nest_out: float32 [4, 32, 128, 128], P('nests', 'tiles')
Inputs may be any that keep to these rules, and one draw needn't show every extreme that they name: nest_pos[n] = (3 i + a, 3 q + c) with a, c in 0..2, i <= 499, and n * 256 <= q <= (n + 1) * 256 - 64: nest n reads and feeds only parent columns of the n-th group of 256 columns.
All inputs are finite; a program needn't handle non-finite values.
Results may differ from a plain program's by a relative error of at most 0.0003.
Values sent between devices are 32-bit elements; how exact they have to be, the bound alone decides.
A program may use at most 128 MiB of HBM per device.

v0:
```python
import jax
import jax.numpy as jnp
from jax import lax
from jax.sharding import PartitionSpec as P

BLK = 64
STEPS = 3


KAPPA = 0.125
HIGH = lax.Precision.HIGHEST


def with_halo(block, sides, width):
    for axis, dim in sides:
        count = lax.axis_size(axis)
        forward = [(i, i + 1) for i in range(count - 1)]
        backward = [(target, source) for source, target in forward]
        low = lax.ppermute(
            lax.slice_in_dim(block, block.shape[dim] - width, None, axis=dim), axis, forward
        )
        high = lax.ppermute(lax.slice_in_dim(block, 0, width, axis=dim), axis, backward)
        block = jnp.concatenate([low, block, high], axis=dim)
    return block


def passed_along(block, axis, distance):
    devices = range(lax.axis_size(axis))
    route = [(i - distance, i) for i in devices if i - distance in devices]
    return lax.ppermute(block, axis, route)


def nest_advance(current, upper, edge, courant, nest_mix):
    left = jnp.concatenate([edge, current[:, :-1]], axis=1)
    mixed = jnp.einsum("xyc,cd->xyd", current, nest_mix, precision=HIGH)
    return current + courant[0] * (upper - current) + courant[1] * (left - current) + mixed


def bilinear(data, anchor, rows, columns_count, block_len):
    cols = jnp.arange(columns_count, dtype=jnp.int32)
    spot = anchor[1] + cols
    near = spot // 3 - anchor[1] // 3
    frac_y = (spot % 3).astype(jnp.float32) / 3.0
    places = jnp.arange(block_len, dtype=jnp.int32)[None, :]
    zero = jnp.zeros((columns_count, block_len), jnp.float32)
    table = jnp.where(places == near[:, None], (1.0 - frac_y)[:, None] + zero, zero)
    table = table + jnp.where(places == near[:, None] + 1, frac_y[:, None] + zero, zero)
    frac_x = ((anchor[0] + rows) % 3).astype(jnp.float32) / 3.0
    upper_part = jnp.einsum("nb,xbc->xnc", table, data[:, 0], precision=HIGH)
    lower_part = jnp.einsum("nb,xbc->xnc", table, data[:, 1], precision=HIGH)
    return (1.0 - frac_x)[:, None, None] * upper_part + frac_x[:, None, None] * lower_part


def shards(parent, nest_state, parent_mix, nest_mix, courant, nest_pos):
    tile_rows, tile_cols, width = parent.shape
    nest_rows = nest_state.shape[1]
    nest_cols = nest_state.shape[2]
    tiles_count = lax.axis_size("tiles")
    slots = (nest_rows + 1) // 3 + 2
    tile_index = lax.axis_index("tiles")
    column_index = lax.axis_index("nests")
    anchor = nest_pos[0]
    corner = anchor[1] // 3
    base = tile_index * nest_rows
    lowest = (anchor[0] + base) // 3
    strip = lax.dynamic_slice_in_dim(parent, corner - column_index * tile_cols, BLK, 1)
    receivers = jnp.arange(tiles_count, dtype=jnp.int32)
    wanted = ((anchor[0] + receivers * nest_rows) // 3)[:, None] + jnp.arange(
        slots, dtype=jnp.int32
    )[None, :]
    local = wanted - tile_index * tile_rows
    inside = (local >= 0) & (local < tile_rows)
    taken = strip[jnp.clip(local, 0, tile_rows - 1)]
    local_rows = lax.psum_scatter(
        jnp.where(inside[..., None, None], taken, 0.0), "tiles", scatter_dimension=0, tiled=True
    ).reshape(slots, BLK, width)
    padded = with_halo(parent, (("tiles", 0), ("nests", 1)), 1)
    beside_all = padded[2:, 1:-1] + padded[:-2, 1:-1] + padded[1:-1, 2:] + padded[1:-1, :-2]
    mixed = jnp.einsum("xyc,cd->xyd", parent, parent_mix, precision=HIGH)
    parent_new = parent + KAPPA * (beside_all - 4.0 * parent) + mixed
    rows = base + jnp.arange(nest_rows, dtype=jnp.int32)
    near_row = (anchor[0] + rows) // 3 - lowest
    data = jnp.stack([local_rows[near_row], local_rows[near_row + 1]], axis=1)
    interp = bilinear(data, anchor, rows, nest_cols, BLK)
    start = 0.5 * (nest_state[0] + interp)
    first = tile_index == 0
    edge = start[:, :1]
    current = start
    for step in range(STEPS):
        above = passed_along(current[-1:], "tiles", 1)
        above = jnp.where(first, start[:1], above)
        upper = jnp.concatenate([above, current[:-1]], axis=0)
        current = nest_advance(current, upper, edge, courant, nest_mix)
    fb_rows = (nest_rows + 2) // 3
    fb_cols = (nest_cols + 2) // 3
    counter = jnp.arange(fb_rows, dtype=jnp.int32)
    ys = -anchor[1] % 3 + 3 * jnp.arange(fb_cols, dtype=jnp.int32)
    col_live = ys < nest_cols
    xs = base + -(anchor[0] + base) % 3 + 3 * counter
    row_live = xs < base + nest_rows
    own_values = current[jnp.clip(xs - base, 0, nest_rows - 1)][:, jnp.clip(ys, 0, nest_cols - 1)]
    own_values = jnp.where((row_live[:, None] & col_live[None, :])[..., None], own_values, 0.0)
    pcol = (anchor[1] + ys) // 3 - column_index * tile_cols
    col_ok = col_live & (pcol >= 0) & (pcol < tile_cols)
    piece = lax.all_gather(own_values, "tiles", axis=0, tiled=True)
    slot_index = jnp.arange(piece.shape[0], dtype=jnp.int32)
    sender = slot_index // fb_rows
    sender_base = sender * nest_rows
    sender_x = sender_base + -(anchor[0] + sender_base) % 3 + 3 * (slot_index % fb_rows)
    prow = (anchor[0] + sender_x) // 3 - tile_index * tile_rows
    row_ok = (sender_x < sender_base + nest_rows) & (prow >= 0) & (prow < tile_rows)
    valid = row_ok[:, None] & col_ok[None, :]
    old = parent_new[
        jnp.clip(prow, 0, tile_rows - 1)[:, None], jnp.clip(pcol, 0, tile_cols - 1)[None, :]
    ]
    diff = jnp.where(valid[..., None], 0.5 * (piece - old), 0.0)
    row_index = jnp.where(valid, prow[:, None], tile_rows)
    col_index = jnp.broadcast_to(jnp.clip(pcol, 0, tile_cols - 1)[None, :], valid.shape)
    parent_out = parent_new.at[row_index, col_index].add(diff, mode="drop")
    return (parent_out, current[None])


def solution(mesh):
    placed = (
        P("tiles", "nests", None),
        P("nests", "tiles", None, None),
        P(),
        P(),
        P(),
        P("nests", None),
    )
    return jax.shard_map(
        shards,
        mesh=mesh,
        in_specs=placed,
        out_specs=(P("tiles", "nests", None), P("nests", "tiles", None, None)),
        check_vma=False,
    )
```

profile of v0, /device:TPU:1, one launch (start us, length us, event | category | flops | bytes accessed | tf_op | source)
XLA Modules:
  0.0 258.9 jit_solution(7235859565456572296)
XLA Ops:
  7.2 1.0 fusion.74
  8.2 4.0 %collective-permute-start.1 = (f32[1,256,128]{2,1,0:T(8,128)S(1)}, f32[1,256,128]{2,1,0:T(8,128)S(1)}, u32[]{:S(2)}, u32[]{:S(2)}) collective-permute-start(f32[1,256,128]{2,1,0:T(8,128)S(1)} %get-tuple-element.13), channel_id=1, source_target_pairs={{0,4},{4,8},{8,12},{12,16},{16,20},{20,24},{24,28},{1,5},{5,9},{9,... | collective-permute-start | bytes 393224 | tf_op jit(solution)/shard_map/ppermute | solution.py:19
  12.2 1.3 collective-permute-start
  13.5 1.3 fusion.75
  17.1 0.7 and_select_fusion.3
  17.8 0.1 compare_select_fusion.1
  17.9 2.0 constant_dynamic-slice_fusion
  19.9 0.1 reshape.529
  20.0 0.6 gather_fusion
  20.6 1.0 broadcast_select_fusion
  21.7 0.6 clamp_shift-left_fusion.2
  22.3 0.7 fusion.61
  23.0 0.6 compare_and_fusion
  24.2 0.7 broadcast_subtract_fusion.1
  24.9 0.6 fusion.55
  25.4 0.6 broadcast_add_fusion
  26.1 0.7 compare_and_fusion.1
  26.7 0.7 fusion.56
  27.7 0.1 fusion.43
  27.8 0.1 reshape.573
  27.9 0.1 reshape.567
  28.0 0.7 constant_dynamic-update-slice_fusion.2
  28.7 7.7 %constant_dynamic-update-slice_fusion.1 = f32[66,256,128]{2,1,0:T(8,128)} fusion(f32[66,256,128]{2,1,0:T(8,128)} %constant_dynamic-update-slice_fusion.2, f32[64,256,128]{2,1,0:T(8,128)} %param.6), kind=kLoop, calls=%fused_computation.84 | loop fusion | bytes 16777216
  36.4 48.9 %reduce-scatter.2.cloned.1.call-done = f32[1,3,64,128]{3,2,1,0:T(8,128)} async-done(((f32[8,3,64,128]{3,2,1,0:T(8,128)}), f32[1,3,64,128]{3,2,1,0:T(8,128)}) %reduce-scatter.2.cloned.1.call-update) | async-done | bytes 98320 | tf_op jit(solution)/shard_map/reduce_scatter | solution.py:74
  85.2 1.4 gather_fusion.1
  86.7 1.4 gather_fusion.2
  88.1 0.4 convolution_multiply_fusion.1
  88.6 0.5 fusion.10
  89.1 2.6 %collective-permute-start.4 = (f32[1,128,128]{2,1,0:T(8,128)S(1)}, f32[1,128,128]{2,1,0:T(8,128)S(1)}, u32[]{:S(2)}, u32[]{:S(2)}) collective-permute-start(f32[1,128,128]{2,1,0:T(8,128)S(1)} %slice.131), channel_id=1, source_target_pairs={{0,4},{4,8},{8,12},{12,16},{16,20},{20,24},{24,28},{1,5},{5,9},{9,... | collective-permute-start | bytes 196616 | tf_op jit(solution)/shard_map/ppermute | solution.py:30
  91.7 0.7 constant_dynamic-update-slice_fusion
  92.4 0.6 collective-permute-done.4
  93.0 0.4 convolution_add_fusion.2
  93.4 3.7 %collective-permute-start.5 = (f32[1,128,128]{2,1,0:T(8,128)S(1)}, f32[1,128,128]{2,1,0:T(8,128)S(1)}, u32[]{:S(2)}, u32[]{:S(2)}) collective-permute-start(f32[1,128,128]{2,1,0:T(8,128)S(1)} %slice.135), channel_id=1, source_target_pairs={{0,4},{4,8},{8,12},{12,16},{16,20},{20,24},{24,28},{1,5},{5,9},{9,... | collective-permute-start | bytes 196616 | tf_op jit(solution)/shard_map/ppermute | solution.py:30
  97.1 1.1 fusion.73
  98.2 7.1 %collective-permute-start.3 = (f32[66,1,128]{2,1,0:T(1,128)S(1)}, f32[66,1,128]{2,1,0:T(1,128)S(1)}, u32[]{:S(2)}, u32[]{:S(2)}) collective-permute-start(f32[66,1,128]{2,1,0:T(1,128)S(1)} %get-tuple-element.11), channel_id=1, source_target_pairs={{0,1},{1,2},{2,3},{4,5},{5,6},{6,7},{8,9},{9,10},{10,11},{12,13},{... | collective-permute-start | bytes 101384 | tf_op jit(solution)/shard_map/ppermute | solution.py:19
  105.3 1.9 collective-permute-start.2
  107.3 0.4 convolution_add_fusion.1
  107.7 4.1 %collective-permute-start.6 = (f32[1,128,128]{2,1,0:T(8,128)S(1)}, f32[1,128,128]{2,1,0:T(8,128)S(1)}, u32[]{:S(2)}, u32[]{:S(2)}) collective-permute-start(f32[1,128,128]{2,1,0:T(8,128)S(1)} %slice.138), channel_id=1, source_target_pairs={{0,4},{4,8},{8,12},{12,16},{16,20},{20,24},{24,28},{1,5},{5,9},{9,... | collective-permute-start | bytes 196616 | tf_op jit(solution)/shard_map/ppermute | solution.py:30
  111.8 27.1 %fusion.4 = f32[64,256,128]{2,1,0:T(8,128)} fusion(f32[64,256,128]{2,1,0:T(8,128)} %param.6, f32[66,256,128]{2,1,0:T(8,128)} %constant_dynamic-update-slice_fusion, f32[66,1,128]{2,1,0:T(1,128)S(1)} %collective-permute-done.3, f32[66,1,128]{2,1,0:T(1,128)S(1)} %collective-permute-done.2, f32[1,256,128]{2,1,0:T(8,128)S(1)} %collective-permute-done.1, ...), kind=kOutput, calls=%fused_computation.12 | convolution fusion | flops 3246391296 | bytes 25823232 | tf_op jit(solution)/shard_map/xyc,cd->xyd/dot_general | solution.py:79
  138.8 7.6 %gather_fusion.5 = f32[688,128]{1,0:T(8,128)S(1)} fusion(f32[64,256,128]{2,1,0:T(8,128)} %fusion.4, s32[688]{0:T(1024)S(1)} %reshape.567), kind=kCustom, calls=%fused_computation.5 | custom fusion | bytes 710016 | tf_op jit(solution)/shard_map/gather | solution.py:113
  146.5 0.4 convolution_add_fusion
  146.9 0.6 gather_fusion.3
  147.5 0.1 copy.11
  147.6 0.6 gather_fusion.4
  148.2 0.1 bitcast_select_fusion
  148.3 25.2 %all_gather.3 = f32[16,43,128]{2,1,0:T(8,128)S(1)} all-gather(f32[2,43,128]{2,1,0:T(8,128)S(1)} %copy.12), channel_id=1, replica_groups=mesh['tiles'=8,'nests'=4] {'tiles'}, dimensions={0}, use_global_device_ids=true | all-gather | bytes 396288 | tf_op jit(solution)/shard_map/all_gather | solution.py:105
  173.6 0.2 multiply_select_fusion
  173.8 78.2 %scatter_fusion = f32[64,256,128]{2,1,0:T(8,128)} fusion(f32[64,256,128]{2,1,0:T(8,128)} %fusion.4, s32[688]{0:T(1024)S(1)} %reshape.573, f32[688,128]{1,0:T(8,128)S(1)} %reshape.575), kind=kCustom, calls=%fused_computation.6 | custom fusion | flops 88064 | bytes 1062272 | tf_op jit(solution)/shard_map/scatter-add | solution.py:119
  (46 shorter events, 0.6 us)
Async XLA Ops:
  7.2 104.6 %copy-start = (f32[128,128]{1,0:T(8,128)S(1)}, f32[128,128]{1,0:T(8,128)}, u32[]{:S(2)}) copy-start(f32[128,128]{1,0:T(8,128)} %param.8) | copy-start | bytes 196612
  7.2 20.3 %copy-start.4 = (f32[2,128]{1,0:T(2,128)S(1)}, f32[2,128]{1,0:T(2,128)}, u32[]{:S(2)}) copy-start(f32[2,128]{1,0:T(2,128)} %param.10) | copy-start | bytes 3076
  7.2 78.0 %reduce-scatter.2.cloned.1.call-start = ((), (), s32[]{:S(2)}) async-start(), calls=%async_computation.1 | async-start | bytes 884736 | tf_op jit(solution)/shard_map/reduce_scatter | solution.py:74
  8.2 19.8 %collective-permute-start.1 = (f32[1,256,128]{2,1,0:T(8,128)S(1)}, f32[1,256,128]{2,1,0:T(8,128)S(1)}, u32[]{:S(2)}, u32[]{:S(2)}) collective-permute-start(f32[1,256,128]{2,1,0:T(8,128)S(1)} %get-tuple-element.13), channel_id=1, source_target_pairs={{0,4},{4,8},{8,12},{12,16},{16,20},{20,24},{24,28},{1,5},{5,9},{9,... | collective-permute-start | bytes 393224 | tf_op jit(solution)/shard_map/ppermute | solution.py:19
  12.2 79.5 %collective-permute-start = (f32[1,256,128]{2,1,0:T(8,128)S(1)}, f32[1,256,128]{2,1,0:T(8,128)S(1)}, u32[]{:S(2)}, u32[]{:S(2)}) collective-permute-start(f32[1,256,128]{2,1,0:T(8,128)S(1)} %get-tuple-element.12), channel_id=1, source_target_pairs={{4,0},{8,4},{12,8},{16,12},{20,16},{24,20},{28,24},{5,1},{9,5},{13... | collective-permute-start | bytes 393224 | tf_op jit(solution)/shard_map/ppermute | solution.py:22
  28.7 59.9 %copy-start.3 = (f32[1,4,128,128]{3,2,1,0:T(8,128)S(1)}, f32[1,4,128,128]{3,2,1,0:T(8,128)}, u32[]{:S(2)}) copy-start(f32[1,4,128,128]{3,2,1,0:T(8,128)} %param.7) | copy-start | bytes 786436
  28.7 64.3 %copy-start.1 = (f32[128,128]{1,0:T(8,128)S(1)}, f32[128,128]{1,0:T(8,128)}, u32[]{:S(2)}) copy-start(f32[128,128]{1,0:T(8,128)} %param.9) | copy-start | bytes 196612
  89.1 3.9 %collective-permute-start.4 = (f32[1,128,128]{2,1,0:T(8,128)S(1)}, f32[1,128,128]{2,1,0:T(8,128)S(1)}, u32[]{:S(2)}, u32[]{:S(2)}) collective-permute-start(f32[1,128,128]{2,1,0:T(8,128)S(1)} %slice.131), channel_id=1, source_target_pairs={{0,4},{4,8},{8,12},{12,16},{16,20},{20,24},{24,28},{1,5},{5,9},{9,... | collective-permute-start | bytes 196616 | tf_op jit(solution)/shard_map/ppermute | solution.py:30
  93.4 13.8 %collective-permute-start.5 = (f32[1,128,128]{2,1,0:T(8,128)S(1)}, f32[1,128,128]{2,1,0:T(8,128)S(1)}, u32[]{:S(2)}, u32[]{:S(2)}) collective-permute-start(f32[1,128,128]{2,1,0:T(8,128)S(1)} %slice.135), channel_id=1, source_target_pairs={{0,4},{4,8},{8,12},{12,16},{16,20},{20,24},{24,28},{1,5},{5,9},{9,... | collective-permute-start | bytes 196616 | tf_op jit(solution)/shard_map/ppermute | solution.py:30
  98.2 13.6 %collective-permute-start.3 = (f32[66,1,128]{2,1,0:T(1,128)S(1)}, f32[66,1,128]{2,1,0:T(1,128)S(1)}, u32[]{:S(2)}, u32[]{:S(2)}) collective-permute-start(f32[66,1,128]{2,1,0:T(1,128)S(1)} %get-tuple-element.11), channel_id=1, source_target_pairs={{0,1},{1,2},{2,3},{4,5},{5,6},{6,7},{8,9},{9,10},{10,11},{12,13},{... | collective-permute-start | bytes 101384 | tf_op jit(solution)/shard_map/ppermute | solution.py:19
  105.3 6.5 %collective-permute-start.2 = (f32[66,1,128]{2,1,0:T(1,128)S(1)}, f32[66,1,128]{2,1,0:T(1,128)S(1)}, u32[]{:S(2)}, u32[]{:S(2)}) collective-permute-start(f32[66,1,128]{2,1,0:T(1,128)S(1)} %get-tuple-element.10), channel_id=1, source_target_pairs={{1,0},{2,1},{3,2},{5,4},{6,5},{7,6},{9,8},{10,9},{11,10},{13,12},{... | collective-permute-start | bytes 101384 | tf_op jit(solution)/shard_map/ppermute | solution.py:22
  107.7 38.8 %collective-permute-start.6 = (f32[1,128,128]{2,1,0:T(8,128)S(1)}, f32[1,128,128]{2,1,0:T(8,128)S(1)}, u32[]{:S(2)}, u32[]{:S(2)}) collective-permute-start(f32[1,128,128]{2,1,0:T(8,128)S(1)} %slice.138), channel_id=1, source_target_pairs={{0,4},{4,8},{8,12},{12,16},{16,20},{20,24},{24,28},{1,5},{5,9},{9,... | collective-permute-start | bytes 196616 | tf_op jit(solution)/shard_map/ppermute | solution.py:30
  146.9 105.2 %copy-start.2 = (f32[4,128,128]{2,1,0:T(8,128)}, f32[4,128,128]{2,1,0:T(8,128)S(1)}, u32[]{:S(2)}) copy-start(f32[4,128,128]{2,1,0:T(8,128)S(1)} %convolution_add_fusion) | copy-start | bytes 786436
Sparse Core Ops, SparseCore 0:
  21.8 63.4 reduce-scatter.1
where the time goes:
time: 263 us; the launch traced here: 259 us
  other arithmetic  85.7 us (33%)
  waiting for transfers between devices  49.5 us (19%)
  matrix products  29.1 us (11%)
  local copies, waits for them, and re-layouts  27.2 us (10%)
  blocking collectives  25.2 us (10%)
  starting transfers between devices  24.7 us (9%)
  between operations  17.6 us (7%)
    scatter-add x1, other arithmetic, shards(): parent_out = parent_new.at[row_index, col_index].add(diff, mode='drop')  78.2 us
    reduce_scatter x1, waiting for transfers between devices, shards(): lax.psum_scatter(jnp.where(inside[..., None, None], taken, 0.0), 'tiles',...  48.9 us
    dot_general x1, matrix products, shards(): mixed = jnp.einsum('xyc,cd->xyd', parent, parent_mix, precision=HIGH)  27.1 us
    all_gather x1, blocking collectives, shards(): piece = lax.all_gather(own_values, 'tiles', axis=0, tiled=True)  25.2 us
    ppermute x2, starting transfers between devices, with_halo(): lax.ppermute(lax.slice_in_dim(block, block.shape[dim] - width, None, axis...  11.1 us
    ppermute x3, starting transfers between devices, passed_along(): return lax.ppermute(block, axis, route)  10.4 us
    unnamed x12, local copies, waits for them, and re-layouts  8.39 us
    gather x2, local copies, waits for them, and re-layouts, shards(): parent_new[jnp.clip(prow, 0, tile_rows - 1)[:, None], jnp.clip(pcol, 0, t...  7.62 us
  transfers between devices with their start and end apart: 8, of which 2 were waited for; matrix products, arithmetic and copies ran while one was open for 23% of the time, Pallas kernels for 0%

commit v1 on v0

v1 whole, which is shorter than its diff:
```python
import functools

import jax
import jax.numpy as jnp
from jax import lax
from jax.experimental import pallas as pl
from jax.experimental.pallas import tpu as pltpu
from jax.sharding import PartitionSpec as P

STEPS = 3
KAPPA = 0.125
HIGH = lax.Precision.HIGHEST
MESH = pl.DeviceIdType.MESH
LANES = 8
ROWS = 8
VMEM_LIMIT = 48 * 1024 * 1024


def split_operator(mix):
    high = mix.astype(jnp.bfloat16)
    low = (mix - high.astype(jnp.float32)).astype(jnp.bfloat16)
    upper = jnp.concatenate([high, low], axis=1)
    lower = jnp.concatenate([high, jnp.zeros_like(low)], axis=1)
    return jnp.concatenate([upper, lower], axis=0)


def apply_operator(values, operator):
    width = values.shape[-1]
    high = values.astype(jnp.bfloat16)
    low = (values - high.astype(jnp.float32)).astype(jnp.bfloat16)
    both = jnp.dot(
        jnp.concatenate([high, low], axis=1), operator, preferred_element_type=jnp.float32
    )
    return both[:, :width] + both[:, width:]


def hat(distance):
    return jnp.maximum(3 - jnp.abs(distance), 0).astype(jnp.float32) * (1.0 / 3.0)


def exchange_kernel(
    nt, nn, lo_count, pos, band, state, edges, mix, courant, parent,
    nest_out, feed, above, below, beside,
    arrived, reduced, rows, halo, start, current,
    send1, recv1, send2, recv2, send3, recv3, send4, recv4,
):
    t = lax.axis_index("tiles")
    n = lax.axis_index("nests")
    nest_rows, nest_cols, width = state.shape
    win = band.shape[0]
    groups = band.shape[1] // LANES
    count = rows.shape[1]
    relay0 = (nt - groups) // 2
    tile_rows = parent.shape[0]

    def low_row(tile):
        return jnp.clip((tile * nest_rows - STEPS + 3) // 3 - 1, 0, win - count)

    def remote(src, dst, send, recv, tile, nest):
        return pltpu.make_async_remote_copy(
            src_ref=src, dst_ref=dst, send_sem=send, recv_sem=recv,
            device_id=(tile, nest), device_id_type=MESH,
        )

    barrier = pltpu.get_barrier_semaphore()
    for step in range(1, nt):
        pl.semaphore_signal(
            barrier, inc=1, device_id=(lax.rem(t + step, nt), n), device_id_type=MESH
        )

    @pl.when(n > 0)
    def _():
        pl.semaphore_signal(barrier, inc=1, device_id=(t, n - 1), device_id_type=MESH)

    @pl.when(n < nn - 1)
    def _():
        pl.semaphore_signal(barrier, inc=1, device_id=(t, n + 1), device_id_type=MESH)

    peers = nt - 1 + (n > 0).astype(jnp.int32) + (n < nn - 1).astype(jnp.int32)
    pl.semaphore_wait(barrier, peers)

    def gather_copy(g):
        return remote(
            band.at[:, pl.ds(g * LANES, LANES)], arrived.at[t], send1.at[g], recv1.at[t],
            relay0 + g, n,
        )

    for g in range(groups):
        @pl.when(t != relay0 + g)
        def _():
            gather_copy(g).start()

    def halo_copy():
        return remote(
            state.at[pl.ds(nest_rows - STEPS, STEPS)], halo, send3.at[0], recv3.at[0], t + 1, n
        )

    def down_copy():
        return remote(parent.at[tile_rows - 1], above, send3.at[1], recv3.at[1], t + 1, n)

    def up_copy():
        return remote(parent.at[0], below, send3.at[2], recv3.at[2], t - 1, n)

    def right_copy():
        return remote(edges.at[1], beside.at[0], send3.at[3], recv3.at[3], t, n + 1)

    def left_copy():
        return remote(edges.at[0], beside.at[1], send3.at[4], recv3.at[4], t, n - 1)

    @pl.when(t < nt - 1)
    def _():
        halo_copy().start()
        down_copy().start()

    @pl.when(t > 0)
    def _():
        up_copy().start()

    @pl.when(n < nn - 1)
    def _():
        right_copy().start()

    @pl.when(n > 0)
    def _():
        left_copy().start()

    @pl.when(t == 0)
    def _():
        halo[...] = jnp.zeros_like(halo)
        above[...] = jnp.zeros_like(above)

    @pl.when(t == nt - 1)
    def _():
        below[...] = jnp.zeros_like(below)

    @pl.when(n == 0)
    def _():
        beside[0] = jnp.zeros(beside.shape[1:], jnp.float32)

    @pl.when(n == nn - 1)
    def _():
        beside[1] = jnp.zeros(beside.shape[1:], jnp.float32)

    is_relay = (t >= relay0) & (t < relay0 + groups)

    def spread_copy(r):
        return remote(
            reduced.at[pl.ds(low_row(r), count)], rows.at[t - relay0], send2.at[r],
            recv2.at[t - relay0], r, n,
        )

    def arrive_copy(s):
        return remote(
            band.at[:, pl.ds(0, LANES)], arrived.at[s], send1.at[0], recv1.at[s], s, n
        )

    for g in range(groups):
        @pl.when(t == relay0 + g)
        def _():
            reduced[...] = band[:, g * LANES:(g + 1) * LANES]

    for s in range(nt):
        @pl.when(is_relay & (t != s))
        def _():
            arrive_copy(s).wait_recv()
            reduced[...] += arrived[s]

    for r in range(nt):
        @pl.when(is_relay & (t != r))
        def _():
            spread_copy(r).start()

    for g in range(groups):
        @pl.when(t == relay0 + g)
        def _():
            rows[g] = reduced[pl.ds(low_row(t), count)]

    operator = split_operator(mix[...])
    shift_x = lax.rem(pos[0, 0], 3)
    shift_y = lax.rem(pos[0, 1], 3)
    span = (nest_cols, groups * LANES)
    table = hat(
        shift_y + lax.broadcasted_iota(jnp.int32, span, 0)
        - 3 * lax.broadcasted_iota(jnp.int32, span, 1)
    )
    first = t == 0

    @pl.when(t > 0)
    def _():
        halo_copy().wait_recv()

    for g in range(groups):
        @pl.when(t != relay0 + g)
        def _():
            remote(
                reduced.at[pl.ds(0, count)], rows.at[g], send2.at[0], recv2.at[g], t, n
            ).wait_recv()

    lines = [
        jnp.dot(
            table, rows[:, i].reshape(groups * LANES, width),
            precision=HIGH, preferred_element_type=jnp.float32,
        )
        for i in range(count)
    ]
    base = t * nest_rows
    lowest = low_row(t)
    total = nest_rows + STEPS
    for k in range(total):
        interp = None
        for i in range(count):
            weight = hat(shift_x + base - STEPS + k - 3 * (lowest + i))
            term = weight * lines[i]
            interp = term if interp is None else interp + term
        own = halo[k] if k < STEPS else state[k - STEPS]
        value = 0.5 * (own + interp)
        start[k] = value
        current[k] = value

    along_x = courant[0:1]
    along_y = courant[1:2]
    at_edge = lax.broadcasted_iota(jnp.int32, (nest_cols, width), 0) == 0
    for step in range(STEPS):
        for k in range(total - 1, step, -1):
            value = current[k]
            upper = current[k - 1]
            if k == STEPS:
                upper = jnp.where(first, start[k], upper)
            left = jnp.where(at_edge, start[k, 0:1], pltpu.roll(value, 1, 0))
            current[k] = (
                value + along_x * (upper - value) + along_y * (left - value)
                + apply_operator(value, operator)
            )

    lead_x = lax.rem(3 - lax.rem(shift_x + base, 3), 3)
    lead_y = lax.rem(3 - shift_y, 3)
    cells = feed.shape[2]
    pick = (
        lax.broadcasted_iota(jnp.int32, (cells, nest_cols), 1)
        == lead_y + 3 * lax.broadcasted_iota(jnp.int32, (cells, nest_cols), 0)
    ).astype(jnp.float32)
    r0, r1, r2, r3 = (current[STEPS + i] for i in range(nest_rows))
    chosen = jnp.where(lead_x == 0, r0, jnp.where(lead_x == 1, r1, r2))
    feed[t, 0] = jnp.dot(pick, chosen, precision=HIGH, preferred_element_type=jnp.float32)
    feed[t, 1] = jnp.dot(pick, r3, precision=HIGH, preferred_element_type=jnp.float32)

    hi_count = nt // lo_count
    hi, lo = t // lo_count, lax.rem(t, lo_count)

    def feed_copy(source, target, slot):
        return remote(feed.at[source], feed.at[source], send4.at[slot], recv4.at[source], target, n)

    sends = []
    for step in range(1, hi_count):
        sends.append(feed_copy(t, lax.rem(hi + step, hi_count) * lo_count + lo, len(sends)))
        sends[-1].start()
    for step in range(1, lo_count):
        sends.append(feed_copy(t, hi * lo_count + lax.rem(lo + step, lo_count), len(sends)))
        sends[-1].start()

    nest_out[...] = current[STEPS:]

    for step in range(1, hi_count):
        source = lax.rem(hi + step, hi_count) * lo_count + lo
        feed_copy(source, t, 0).wait_recv()
        for across in range(1, lo_count):
            target = hi * lo_count + lax.rem(lo + across, lo_count)
            sends.append(feed_copy(source, target, len(sends)))
            sends[-1].start()
    for across in range(1, lo_count):
        for step in range(hi_count):
            source = lax.rem(hi + step, hi_count) * lo_count + lax.rem(lo + across, lo_count)
            feed_copy(source, t, 0).wait_recv()

    @pl.when(t > 0)
    def _():
        down_copy().wait_recv()

    @pl.when(t < nt - 1)
    def _():
        up_copy().wait_recv()

    @pl.when(n > 0)
    def _():
        right_copy().wait_recv()

    @pl.when(n < nn - 1)
    def _():
        left_copy().wait_recv()

    for copy in sends:
        copy.wait_send()
    for g in range(groups):
        @pl.when(t != relay0 + g)
        def _():
            gather_copy(g).wait_send()
    for r in range(nt):
        @pl.when(is_relay & (t != r))
        def _():
            spread_copy(r).wait_send()

    @pl.when(t < nt - 1)
    def _():
        halo_copy().wait_send()
        down_copy().wait_send()

    @pl.when(t > 0)
    def _():
        up_copy().wait_send()

    @pl.when(n < nn - 1)
    def _():
        right_copy().wait_send()

    @pl.when(n > 0)
    def _():
        left_copy().wait_send()


def parent_kernel(nest_rows, nest_total, nest_cols, place, block, over, under, above, below,
                  beside, mix, feed, out, operator):
    step = pl.program_id(0)
    last = pl.num_programs(0) - 1
    lines, cols, width = block.shape

    @pl.when(step == 0)
    def _():
        operator[...] = split_operator(mix[...])

    column = lax.broadcasted_iota(jnp.int32, (cols, width), 0)
    weights = operator[...]
    for i in range(lines):
        value = block[i]
        if i == 0:
            up = jnp.where(step == 0, above[...], over[0])
        else:
            up = block[i - 1]
        if i == lines - 1:
            down = jnp.where(step == last, below[...], under[0])
        else:
            down = block[i + 1]
        row = step * lines + i
        left = jnp.where(column == 0, beside[0, pl.ds(row, 1)], pltpu.roll(value, 1, 0))
        right = jnp.where(
            column == cols - 1, beside[1, pl.ds(row, 1)], pltpu.roll(value, cols - 1, 0)
        )
        out[i] = (
            value + KAPPA * ((up + down + right + left) - 4.0 * value)
            + apply_operator(value, weights)
        )

    top, lead_x, first_col, lead_y = place[0], place[1], place[2], place[3]
    slots = feed.shape[1]
    cells = feed.shape[2]
    window = cells + 8
    base_col = pl.multiple_of(first_col // 8 * 8, 8)
    offset = first_col - base_col
    limit = (nest_cols - lead_y + 2) // 3
    for i in range(lines):
        x = lead_x + 3 * (step * lines + i - top)

        @pl.when((x >= 0) & (x < nest_total))
        def _():
            sender = x // nest_rows
            slot = (x - sender * nest_rows) // 3
            cell = lax.broadcasted_iota(jnp.int32, (window, width), 0) - offset
            fed = jnp.concatenate([feed[sender, slot], jnp.zeros((8, width), jnp.float32)], axis=0)
            fed = pltpu.roll(fed, offset, 0)
            old = out[i, pl.ds(base_col, window)]
            new = jnp.where((cell >= 0) & (cell < limit), old + 0.5 * (fed - old), old)
            out[i, pl.ds(base_col, window)] = new


def shards(nt, nn, parent, nest_state, parent_mix, nest_mix, courant, nest_pos):
    tile_rows, tile_cols, width = parent.shape
    _, nest_rows, nest_cols, _ = nest_state.shape
    nest_total = nest_rows * nt
    win = (nest_total + 1) // 3 + 2
    need = (nest_cols + 1) // 3 + 2
    span = -(-need // LANES) * LANES
    groups = span // LANES
    count = -(-(nest_rows + STEPS + 1) // 3) + 2
    fb_cols = -(-((nest_cols + 2) // 3) // LANES) * LANES
    lo_count = nt // 4
    slots = (nest_rows + 2) // 3
    t = lax.axis_index("tiles")
    n = lax.axis_index("nests")
    anchor = nest_pos[0]
    local = anchor[0] // 3 - t * tile_rows
    corner = anchor[1] // 3 - n * tile_cols
    begin = jnp.clip(local, 0, tile_rows - win)
    strip = lax.dynamic_slice(parent, (begin, corner, 0), (win, span, width))
    strip = jnp.pad(strip, ((win, win), (0, 0), (0, 0)))
    move = jnp.clip(local - begin, -win, win) + win
    band = lax.dynamic_slice(strip, (move, 0, 0), (win, span, width))
    edges = jnp.stack([parent[:, 0], parent[:, -1]])
    vmem = pl.BlockSpec(memory_space=pltpu.VMEM)
    f32 = jnp.float32
    dma = pltpu.SemaphoreType.DMA
    nest_out, feed, above, below, beside = pl.pallas_call(
        functools.partial(exchange_kernel, nt, nn, lo_count),
        out_shape=(
            jax.ShapeDtypeStruct((nest_rows, nest_cols, width), f32),
            jax.ShapeDtypeStruct((nt, slots, fb_cols, width), f32),
            jax.ShapeDtypeStruct((tile_cols, width), f32),
            jax.ShapeDtypeStruct((tile_cols, width), f32),
            jax.ShapeDtypeStruct((2, tile_rows, width), f32),
        ),
        in_specs=[
            pl.BlockSpec(memory_space=pltpu.SMEM), vmem, vmem, vmem, vmem, vmem,
            pl.BlockSpec(memory_space=pl.ANY),
        ],
        out_specs=(vmem,) * 5,
        scratch_shapes=[
            pltpu.VMEM((nt, win, LANES, width), f32),
            pltpu.VMEM((win, LANES, width), f32),
            pltpu.VMEM((groups, count, LANES, width), f32),
            pltpu.VMEM((STEPS, nest_cols, width), f32),
            pltpu.VMEM((nest_rows + STEPS, nest_cols, width), f32),
            pltpu.VMEM((nest_rows + STEPS, nest_cols, width), f32),
            dma((groups,)), dma((nt,)), dma((nt,)), dma((groups,)),
            dma((5,)), dma((5,)), dma((nt - 1,)), dma((nt,)),
        ],
        compiler_params=pltpu.CompilerParams(
            collective_id=0, has_side_effects=True, vmem_limit_bytes=VMEM_LIMIT
        ),
        name="nest_exchange",
    )(nest_pos, band, nest_state[0], edges, nest_mix, courant, parent)

    lead_x = -anchor[0] % 3
    lead_y = -anchor[1] % 3
    place = jnp.stack([
        (anchor[0] + lead_x) // 3 - t * tile_rows,
        lead_x,
        (anchor[1] + lead_y) // 3 - n * tile_cols,
        lead_y,
    ]).astype(jnp.int32)
    steps = tile_rows // ROWS
    whole = lambda *shape: pl.BlockSpec(shape, lambda i, place: (0,) * len(shape))
    line = (1, tile_cols, width)
    parent_out = pl.pallas_call(
        functools.partial(parent_kernel, nest_rows, nest_total, nest_cols),
        out_shape=jax.ShapeDtypeStruct(parent.shape, f32),
        grid_spec=pltpu.PrefetchScalarGridSpec(
            num_scalar_prefetch=1,
            grid=(steps,),
            in_specs=[
                pl.BlockSpec((ROWS, tile_cols, width), lambda i, place: (i, 0, 0)),
                pl.BlockSpec(line, lambda i, place: (jnp.maximum(i * ROWS - 1, 0), 0, 0)),
                pl.BlockSpec(
                    line, lambda i, place: (jnp.minimum(i * ROWS + ROWS, tile_rows - 1), 0, 0)
                ),
                whole(tile_cols, width),
                whole(tile_cols, width),
                whole(2, tile_rows, width),
                whole(width, width),
                whole(nt, slots, fb_cols, width),
            ],
            out_specs=pl.BlockSpec((ROWS, tile_cols, width), lambda i, place: (i, 0, 0)),
            scratch_shapes=[pltpu.VMEM((2 * width, 2 * width), jnp.bfloat16)],
        ),
        compiler_params=pltpu.CompilerParams(vmem_limit_bytes=VMEM_LIMIT),
        name="parent_step",
    )(place, parent, parent, parent, above, below, beside, parent_mix, feed)
    return parent_out, nest_out[None]


def solution(mesh):
    placed = (
        P("tiles", "nests", None),
        P("nests", "tiles", None, None),
        P(),
        P(),
        P(),
        P("nests", None),
    )
    return jax.shard_map(
        functools.partial(shards, mesh.shape["tiles"], mesh.shape["nests"]),
        mesh=mesh,
        in_specs=placed,
        out_specs=(P("tiles", "nests", None), P("nests", "tiles", None, None)),
        check_vma=False,
    )
```

time: 263 us -> 61.4 us (0.23)
  the two profiles are of different devices: /device:TPU:1 before, /device:TPU:0 now
where the time goes in v1:
time: 61.4 us; the launch traced here: 60.8 us
  Pallas kernels  46.1 us (75%)
  local copies, waits for them, and re-layouts  7.3 us (12%)
  between operations  7.3 us (12%)
    pallas_call x1, Pallas kernels, shards(): pl.pallas_call(functools.partial(exchange_kernel, nt, nn, lo_count), out_...  34.1 us
    pallas_call x1, Pallas kernels, shards(): pl.pallas_call(functools.partial(parent_kernel, nest_rows, nest_total, ne...  12 us
    unnamed x11, local copies, waits for them, and re-layouts  3.82 us
    slice x1, local copies, waits for them, and re-layouts, shards(): anchor[0] + lead_x  1.31 us

profile of v1, /device:TPU:0, one launch (start us, length us, event | category | flops | bytes accessed | tf_op | source)
XLA Modules:
  0.0 60.8 jit_solution(10190615343510655696)
XLA Ops:
  0.6 0.0 copy-start.2
  0.6 1.3 %fusion.1 = (s32[1,1]{1,0:T(1,128)}, s32[1,1]{1,0:T(1,128)}) fusion(s32[1,2]{1,0:T(1,128)} %pos.1), kind=kLoop, calls=%fused_computation.5 | loop fusion | bytes 16 | tf_op jit(solution)/shard_map/slice | solution.py:433
  8.6 0.1 pad_add_fusion.place
  8.6 1.1 %fusion = (f32[64,1,128]{2,1,0:T(1,128)S(1)}, f32[64,1,128]{2,1,0:T(1,128)S(1)}) fusion(f32[64,256,128]{2,1,0:T(8,128)} %under.1), kind=kLoop, calls=%fused_computation.4 | loop fusion | bytes 131072 | tf_op jit(solution)/shard_map/slice | solution.py:396
  9.7 1.0 %constant_dynamic-slice_fusion = f32[13,48,128]{2,1,0:T(8,128)S(1)} fusion(f32[64,256,128]{2,1,0:T(8,128)} %under.1, s32[]{:T(128)S(6)} %min.7, s32[]{:T(128)S(6)} %select_n.37), kind=kLoop, calls=%fused_computation.3 | loop fusion | bytes 638984 | tf_op jit(solution)/shard_map/dynamic_slice | solution.py:392
  10.8 0.0 copy-start
  10.8 0.9 %copy-done = f32[1,4,128,128]{3,2,1,0:T(8,128)S(1)} copy-done((f32[1,4,128,128]{3,2,1,0:T(8,128)S(1)}, f32[1,4,128,128]{3,2,1,0:T(8,128)}, u32[]{:S(2)}) %copy-start) | copy-done | bytes 262168
  11.8 0.0 copy-start.1
  11.8 0.8 %copy-done.1 = f32[128,128]{1,0:T(8,128)S(1)} copy-done((f32[128,128]{1,0:T(8,128)S(1)}, f32[128,128]{1,0:T(8,128)}, u32[]{:S(2)}) %copy-start.1) | copy-done | bytes 65560
  12.6 0.0 copy-start.3
  12.6 0.7 %copy-done.3 = s32[1,2]{1,0:T(1,128)S(1)} copy-done((s32[1,2]{1,0:T(1,128)S(1)}, s32[1,2]{1,0:T(1,128)}, u32[]{:S(2)}) %copy-start.3) | copy-done | bytes 32
  13.3 0.0 copy-start.4
  13.3 0.7 %copy-done.4 = f32[2,128]{1,0:T(2,128)S(1)} copy-done((f32[2,128]{1,0:T(2,128)S(1)}, f32[2,128]{1,0:T(2,128)}, u32[]{:S(2)}) %copy-start.4) | copy-done | bytes 1048
  14.0 34.1 %nest_exchange.1 = (f32[4,128,128]{2,1,0:T(8,128)S(1)}, f32[8,2,48,128]{3,2,1,0:T(8,128)S(1)}, f32[256,128]{1,0:T(8,128)S(1)}, f32[256,128]{1,0:T(8,128)S(1)}, f32[2,64,128]{2,1,0:T(8,128)S(1)}) custom-call(s32[1,2]{1,0:T(1,128)S(1)} %copy-done.3, f32[13,48,128]{2,1,0:T(8,128)S(1)} %pad_dynamic-slice_fusion.band, f32[4,128,128]{2,1,0:T(8,128)S(1)} %bitcast.14, ...), custom_call_target="tpu_custom_call" | custom-call | tf_op jit(solution)/shard_map/nest_exchange/pallas_call | solution.py:400
  48.1 0.0 copy-done.2
  48.1 12.0 %parent_step.1 = f32[64,256,128]{2,1,0:T(8,128)} custom-call(s32[4]{0:T(128)S(1)} %pad_add_fusion.place, f32[64,256,128]{2,1,0:T(8,128)} %under.1, f32[64,256,128]{2,1,0:T(8,128)} %under.1, f32[64,256,128]{2,1,0:T(8,128)} %under.1, f32[256,128]{1,0:T(8,128)S(1)} %get-tuple-element.7.above, f32[256,128]{1,0:T(8,128)S(1)} %get-tuple-element.8.below, ...), custom_call_target="tpu_custom_call" | custom-call | tf_op jit(solution)/shard_map/parent_step/pallas_call | solution.py:441
  60.1 0.7 %copy.13 = f32[1,4,128,128]{3,2,1,0:T(8,128)} copy(f32[1,4,128,128]{3,2,1,0:T(8,128)S(1)} %bitcast.15) | data formatting | bytes 524288
  (2 shorter events, 0.1 us)
Async XLA Ops:
  0.6 47.4 %copy-start.2 = (f32[128,128]{1,0:T(8,128)S(1)}, f32[128,128]{1,0:T(8,128)}, u32[]{:S(2)}) copy-start(f32[128,128]{1,0:T(8,128)} %mix.3) | copy-start | bytes 196612
  10.8 1.0 %copy-start = (f32[1,4,128,128]{3,2,1,0:T(8,128)S(1)}, f32[1,4,128,128]{3,2,1,0:T(8,128)}, u32[]{:S(2)}) copy-start(f32[1,4,128,128]{3,2,1,0:T(8,128)} %param.7) | copy-start | bytes 786436
  11.8 0.8 %copy-start.1 = (f32[128,128]{1,0:T(8,128)S(1)}, f32[128,128]{1,0:T(8,128)}, u32[]{:S(2)}) copy-start(f32[128,128]{1,0:T(8,128)} %mix.2) | copy-start | bytes 196612
  12.6 0.7 %copy-start.3 = (s32[1,2]{1,0:T(1,128)S(1)}, s32[1,2]{1,0:T(1,128)}, u32[]{:S(2)}) copy-start(s32[1,2]{1,0:T(1,128)} %pos.1) | copy-start | bytes 28
  13.3 0.7 %copy-start.4 = (f32[2,128]{1,0:T(2,128)S(1)}, f32[2,128]{1,0:T(2,128)}, u32[]{:S(2)}) copy-start(f32[2,128]{1,0:T(2,128)} %courant.1) | copy-start | bytes 3076

commit v2 on v1

--- a/solution.py
+++ b/solution.py
@@ -13,7 +13,9 @@
 MESH = pl.DeviceIdType.MESH
 LANES = 8
 ROWS = 8
-VMEM_LIMIT = 48 * 1024 * 1024
+CHUNK = 4
+PAD = 8
+VMEM_LIMIT = 56 * 1024 * 1024
 
 
 def split_operator(mix):
@@ -39,19 +41,20 @@
 
 
 def exchange_kernel(
-    nt, nn, lo_count, pos, band, state, edges, mix, courant, parent,
-    nest_out, feed, above, below, beside,
+    nt, nn, lo_count, pos, parent_hbm, state_hbm, pmix_hbm, nmix_hbm, courant_hbm,
+    nest_out, feed, parent_new,
+    held, fresh, band, edges, above, below, beside, state, pmix, nmix, courant,
     arrived, reduced, rows, halo, start, current,
-    send1, recv1, send2, recv2, send3, recv3, send4, recv4,
+    load, store, send1, recv1, send2, recv2, send3, recv3, send4, recv4,
 ):
     t = lax.axis_index("tiles")
     n = lax.axis_index("nests")
     nest_rows, nest_cols, width = state.shape
-    win = band.shape[0]
-    groups = band.shape[1] // LANES
+    tile_rows, tile_cols, _ = fresh.shape
+    win, span, _ = band.shape
+    groups = span // LANES
     count = rows.shape[1]
     relay0 = (nt - groups) // 2
-    tile_rows = parent.shape[0]
 
     def low_row(tile):
         return jnp.clip((tile * nest_rows - STEPS + 3) // 3 - 1, 0, win - count)
@@ -62,6 +65,18 @@
             device_id=(tile, nest), device_id_type=MESH,
         )
 
+    loads = [
+        pltpu.make_async_copy(
+            parent_hbm, held.at[pl.ds(1, tile_rows), pl.ds(PAD, tile_cols)], load.at[0]
+        ),
+        pltpu.make_async_copy(pmix_hbm, pmix, load.at[1]),
+        pltpu.make_async_copy(state_hbm.at[0], state, load.at[2]),
+        pltpu.make_async_copy(nmix_hbm, nmix, load.at[3]),
+        pltpu.make_async_copy(courant_hbm, courant, load.at[4]),
+    ]
+    for copy in loads:
+        copy.start()
+
     barrier = pltpu.get_barrier_semaphore()
     for step in range(1, nt):
         pl.semaphore_signal(
@@ -76,8 +91,65 @@
     def _():
         pl.semaphore_signal(barrier, inc=1, device_id=(t, n + 1), device_id_type=MESH)
 
+    held[0] = jnp.zeros(held.shape[1:], jnp.float32)
+    held[tile_rows + 1] = jnp.zeros(held.shape[1:], jnp.float32)
+    strip = jnp.zeros((tile_rows, PAD, width), jnp.float32)
+    held[1:tile_rows + 1, :PAD] = strip
+    held[1:tile_rows + 1, PAD + tile_cols:] = strip
+
+    @pl.when(t == 0)
+    def _():
+        halo[...] = jnp.zeros_like(halo)
+        above[...] = jnp.zeros_like(above)
+
+    @pl.when(t == nt - 1)
+    def _():
+        below[...] = jnp.zeros_like(below)
+
+    @pl.when(n == 0)
+    def _():
+        beside[0] = jnp.zeros(beside.shape[1:], jnp.float32)
+
+    @pl.when(n == nn - 1)
+    def _():
+        beside[1] = jnp.zeros(beside.shape[1:], jnp.float32)
+
     peers = nt - 1 + (n > 0).astype(jnp.int32) + (n < nn - 1).astype(jnp.int32)
     pl.semaphore_wait(barrier, peers)
+
+    def halo_copy():
+        return remote(
+            state_hbm.at[0, pl.ds(nest_rows - STEPS, STEPS)], halo, send3.at[0], recv3.at[0],
+            t + 1, n,
+        )
+
+    def down_copy():
+        return remote(
+            parent_hbm.at[tile_rows - 1], above, send3.at[1], recv3.at[1], t + 1, n
+        )
+
+    def up_copy():
+        return remote(parent_hbm.at[0], below, send3.at[2], recv3.at[2], t - 1, n)
+
+    def right_copy():
+        return remote(edges.at[1], beside.at[0], send3.at[3], recv3.at[3], t, n + 1)
+
+    def left_copy():
+        return remote(edges.at[0], beside.at[1], send3.at[4], recv3.at[4], t, n - 1)
+
+    @pl.when(t < nt - 1)
+    def _():
+        halo_copy().start()
+
+    loads[0].wait()
+
+    local = pos[0, 0] // 3 - t * tile_rows
+    corner = jnp.clip(pos[0, 1] // 3 - n * tile_cols, 0, tile_cols - span)
+    for w in range(win):
+        row = local + w
+        inside = (row >= 0) & (row < tile_rows)
+        part = held[jnp.clip(row, 0, tile_rows - 1) + 1, pl.ds(PAD + corner, span)]
+        band[w] = jnp.where(inside, part, 0.0)
 
     def gather_copy(g):
         return remote(
@@ -90,31 +162,8 @@
         def _():
             gather_copy(g).start()
 
-    def halo_copy():
-        return remote(
-            state.at[pl.ds(nest_rows - STEPS, STEPS)], halo, send3.at[0], recv3.at[0], t + 1, n
-        )
-
-    def down_copy():
-        return remote(parent.at[tile_rows - 1], above, send3.at[1], recv3.at[1], t + 1, n)
-
-    def up_copy():
-        return remote(parent.at[0], below, send3.at[2], recv3.at[2], t - 1, n)
-
-    def right_copy():
-        return remote(edges.at[1], beside.at[0], send3.at[3], recv3.at[3], t, n + 1)
-
-    def left_copy():
-        return remote(edges.at[0], beside.at[1], send3.at[4], recv3.at[4], t, n - 1)
-
-    @pl.when(t < nt - 1)
-    def _():
-        halo_copy().start()
-        down_copy().start()
-
-    @pl.when(t > 0)
-    def _():
-        up_copy().start()
+    edges[0] = held[1:tile_rows + 1, PAD]
+    edges[1] = held[1:tile_rows + 1, PAD + tile_cols - 1]
 
     @pl.when(n < nn - 1)
     def _():
@@ -124,22 +173,30 @@
     def _():
         left_copy().start()
 
-    @pl.when(t == 0)
-    def _():
-        halo[...] = jnp.zeros_like(halo)
-        above[...] = jnp.zeros_like(above)
-
-    @pl.when(t == nt - 1)
-    def _():
-        below[...] = jnp.zeros_like(below)
-
-    @pl.when(n == 0)
-    def _():
-        beside[0] = jnp.zeros(beside.shape[1:], jnp.float32)
-
-    @pl.when(n == nn - 1)
-    def _():
-        beside[1] = jnp.zeros(beside.shape[1:], jnp.float32)
+    for copy in loads[1:]:
+        copy.wait()
+    parent_operator = split_operator(pmix[...])
+
+    def parent_rows(step, carry):
+        half = tile_cols // 2
+        for i in range(CHUNK):
+            row = step * CHUNK + i
+            for begin in (0, half):
+                at = PAD + begin
+                value = held[row + 1, at:at + half]
+                around = (
+                    held[row, at:at + half] + held[row + 2, at:at + half]
+                    + held[row + 1, at + 1:at + 1 + half] + held[row + 1, at - 1:at - 1 + half]
+                )
+                fresh[row, begin:begin + half] = (
+                    value + KAPPA * (around - 4.0 * value)
+                    + apply_operator(value, parent_operator)
+                )
+        return carry
+
+    chunks = tile_rows // CHUNK
+    marks = [0, chunks // 2, chunks * 11 // 16, chunks * 14 // 16, chunks]
+    lax.fori_loop(marks[0], marks[1], parent_rows, 0)
 
     is_relay = (t >= relay0) & (t < relay0 + groups)
 
@@ -175,7 +232,17 @@
         def _():
             rows[g] = reduced[pl.ds(low_row(t), count)]
 
-    operator = split_operator(mix[...])
+    @pl.when(t < nt - 1)
+    def _():
+        down_copy().start()
+
+    @pl.when(t > 0)
+    def _():
+        up_copy().start()
+
+    lax.fori_loop(marks[1], marks[2], parent_rows, 0)
+
+    operator = split_operator(nmix[...])
     shift_x = lax.rem(pos[0, 0], 3)
     shift_y = lax.rem(pos[0, 1], 3)
     span = (nest_cols, groups * LANES)
@@ -259,6 +326,7 @@
         sends[-1].start()
 
     nest_out[...] = current[STEPS:]
+    lax.fori_loop(marks[2], marks[3], parent_rows, 0)
 
     for step in range(1, hi_count):
         source = lax.rem(hi + step, hi_count) * lo_count + lo
@@ -267,27 +335,37 @@
             target = hi * lo_count + lax.rem(lo + across, lo_count)
             sends.append(feed_copy(source, target, len(sends)))
             sends[-1].start()
+
+    lax.fori_loop(marks[3], marks[4], parent_rows, 0)
+
+    @pl.when(t > 0)
+    def _():
+        down_copy().wait_recv()
+
+    @pl.when(t < nt - 1)
+    def _():
+        up_copy().wait_recv()
+
+    @pl.when(n > 0)
+    def _():
+        right_copy().wait_recv()
+
+    @pl.when(n < nn - 1)
+    def _():
+        left_copy().wait_recv()
+
+    fresh[0] += KAPPA * above[...]
+    fresh[tile_rows - 1] += KAPPA * below[...]
+    fresh[:, 0] += KAPPA * beside[0]
+    fresh[:, tile_cols - 1] += KAPPA * beside[1]
+    out_copy = pltpu.make_async_copy(fresh, parent_new, store.at[0])
+    out_copy.start()
+
     for across in range(1, lo_count):
         for step in range(hi_count):
             source = lax.rem(hi + step, hi_count) * lo_count + lax.rem(lo + across, lo_count)
             feed_copy(source, t, 0).wait_recv()
 
-    @pl.when(t > 0)
-    def _():
-        down_copy().wait_recv()
-
-    @pl.when(t < nt - 1)
-    def _():
-        up_copy().wait_recv()
-
-    @pl.when(n > 0)
-    def _():
-        right_copy().wait_recv()
-
-    @pl.when(n < nn - 1)
-    def _():
-        left_copy().wait_recv()
-
     for copy in sends:
         copy.wait_send()
     for g in range(groups):
@@ -315,42 +393,23 @@
     @pl.when(n > 0)
     def _():
         left_copy().wait_send()
-
-
-def parent_kernel(nest_rows, nest_total, nest_cols, place, block, over, under, above, below,
-                  beside, mix, feed, out, operator):
+    out_copy.wait()
+
+
+def feedback_kernel(nest_rows, nest_total, nest_cols, pos, block, feed, nest, out, nest_out):
     step = pl.program_id(0)
-    last = pl.num_programs(0) - 1
     lines, cols, width = block.shape
+    tile_rows = lines * pl.num_programs(0)
 
     @pl.when(step == 0)
     def _():
-        operator[...] = split_operator(mix[...])
-
-    column = lax.broadcasted_iota(jnp.int32, (cols, width), 0)
-    weights = operator[...]
-    for i in range(lines):
-        value = block[i]
-        if i == 0:
-            up = jnp.where(step == 0, above[...], over[0])
-        else:
-            up = block[i - 1]
-        if i == lines - 1:
-            down = jnp.where(step == last, below[...], under[0])
-        else:
-            down = block[i + 1]
-        row = step * lines + i
-        left = jnp.where(column == 0, beside[0, pl.ds(row, 1)], pltpu.roll(value, 1, 0))
-        right = jnp.where(
-            column == cols - 1, beside[1, pl.ds(row, 1)], pltpu.roll(value, cols - 1, 0)
-        )
-        out[i] = (
-            value + KAPPA * ((up + down + right + left) - 4.0 * value)
-            + apply_operator(value, weights)
-        )
-
-    top, lead_x, first_col, lead_y = place[0], place[1], place[2], place[3]
-    slots = feed.shape[1]
+        nest_out[0] = nest[...]
+
+    out[...] = block[...]
+    lead_x = lax.rem(3 - lax.rem(pos[0, 0], 3), 3)
+    lead_y = lax.rem(3 - lax.rem(pos[0, 1], 3), 3)
+    top = (pos[0, 0] + lead_x) // 3 - lax.axis_index("tiles") * tile_rows
+    first_col = (pos[0, 1] + lead_y) // 3 - lax.axis_index("nests") * cols
     cells = feed.shape[2]
     window = cells + 8
     base_col = pl.multiple_of(first_col // 8 * 8, 8)
@@ -383,41 +442,39 @@
     fb_cols = -(-((nest_cols + 2) // 3) // LANES) * LANES
     lo_count = nt // 4
     slots = (nest_rows + 2) // 3
-    t = lax.axis_index("tiles")
-    n = lax.axis_index("nests")
-    anchor = nest_pos[0]
-    local = anchor[0] // 3 - t * tile_rows
-    corner = anchor[1] // 3 - n * tile_cols
-    begin = jnp.clip(local, 0, tile_rows - win)
-    strip = lax.dynamic_slice(parent, (begin, corner, 0), (win, span, width))
-    strip = jnp.pad(strip, ((win, win), (0, 0), (0, 0)))
-    move = jnp.clip(local - begin, -win, win) + win
-    band = lax.dynamic_slice(strip, (move, 0, 0), (win, span, width))
-    edges = jnp.stack([parent[:, 0], parent[:, -1]])
     vmem = pl.BlockSpec(memory_space=pltpu.VMEM)
+    smem = pl.BlockSpec(memory_space=pltpu.SMEM)
+    hbm = pl.BlockSpec(memory_space=pl.ANY)
     f32 = jnp.float32
     dma = pltpu.SemaphoreType.DMA
-    nest_out, feed, above, below, beside = pl.pallas_call(
+    nest_new, feed, parent_new = pl.pallas_call(
         functools.partial(exchange_kernel, nt, nn, lo_count),
         out_shape=(
             jax.ShapeDtypeStruct((nest_rows, nest_cols, width), f32),
             jax.ShapeDtypeStruct((nt, slots, fb_cols, width), f32),
-            jax.ShapeDtypeStruct((tile_cols, width), f32),
-            jax.ShapeDtypeStruct((tile_cols, width), f32),
-            jax.ShapeDtypeStruct((2, tile_rows, width), f32),
+            jax.ShapeDtypeStruct(parent.shape, f32),
         ),
-        in_specs=[
-            pl.BlockSpec(memory_space=pltpu.SMEM), vmem, vmem, vmem, vmem, vmem,
-            pl.BlockSpec(memory_space=pl.ANY),
-        ],
-        out_specs=(vmem,) * 5,
+        in_specs=[smem] + [hbm] * 5,
+        out_specs=(vmem, vmem, hbm),
         scratch_shapes=[
+            pltpu.VMEM((tile_rows + 2, tile_cols + 2 * PAD, width), f32),
+            pltpu.VMEM((tile_rows, tile_cols, width), f32),
+            pltpu.VMEM((win, span, width), f32),
+            pltpu.VMEM((2, tile_rows, width), f32),
+            pltpu.VMEM((tile_cols, width), f32),
+            pltpu.VMEM((tile_cols, width), f32),
+            pltpu.VMEM((2, tile_rows, width), f32),
+            pltpu.VMEM((nest_rows, nest_cols, width), f32),
+            pltpu.VMEM((width, width), f32),
+            pltpu.VMEM((width, width), f32),
+            pltpu.VMEM((2, width), f32),
             pltpu.VMEM((nt, win, LANES, width), f32),
             pltpu.VMEM((win, LANES, width), f32),
             pltpu.VMEM((groups, count, LANES, width), f32),
             pltpu.VMEM((STEPS, nest_cols, width), f32),
             pltpu.VMEM((nest_rows + STEPS, nest_cols, width), f32),
             pltpu.VMEM((nest_rows + STEPS, nest_cols, width), f32),
+            dma((5,)), dma((1,)),
             dma((groups,)), dma((nt,)), dma((nt,)), dma((groups,)),
             dma((5,)), dma((5,)), dma((nt - 1,)), dma((nt,)),
         ],
@@ -425,44 +482,25 @@
             collective_id=0, has_side_effects=True, vmem_limit_bytes=VMEM_LIMIT
         ),
         name="nest_exchange",
-    )(nest_pos, band, nest_state[0], edges, nest_mix, courant, parent)
-
-    lead_x = -anchor[0] % 3
-    lead_y = -anchor[1] % 3
-    place = jnp.stack([
-        (anchor[0] + lead_x) // 3 - t * tile_rows,
-        lead_x,
-        (anchor[1] + lead_y) // 3 - n * tile_cols,
-        lead_y,
-    ]).astype(jnp.int32)
-    steps = tile_rows // ROWS
-    whole = lambda *shape: pl.BlockSpec(shape, lambda i, place: (0,) * len(shape))
-    line = (1, tile_cols, width)
-    parent_out = pl.pallas_call(
-        functools.partial(parent_kernel, nest_rows, nest_total, nest_cols),
-        out_shape=jax.ShapeDtypeStruct(parent.shape, f32),
-        grid_spec=pltpu.PrefetchScalarGridSpec(
-            num_scalar_prefetch=1,
-            grid=(steps,),
-            in_specs=[
-                pl.BlockSpec((ROWS, tile_cols, width), lambda i, place: (i, 0, 0)),
-                pl.BlockSpec(line, lambda i, place: (jnp.maximum(i * ROWS - 1, 0), 0, 0)),
-                pl.BlockSpec(
-                    line, lambda i, place: (jnp.minimum(i * ROWS + ROWS, tile_rows - 1), 0, 0)
-                ),
-                whole(tile_cols, width),
-                whole(tile_cols, width),
-                whole(2, tile_rows, width),
-                whole(width, width),
-                whole(nt, slots, fb_cols, width),
-            ],
-            out_specs=pl.BlockSpec((ROWS, tile_cols, width), lambda i, place: (i, 0, 0)),
-            scratch_shapes=[pltpu.VMEM((2 * width, 2 * width), jnp.bfloat16)],
+    )(nest_pos, parent, nest_state, parent_mix, nest_mix, courant)
+
+    lines = pl.BlockSpec((ROWS, tile_cols, width), lambda i: (i, 0, 0))
+    return pl.pallas_call(
+        functools.partial(feedback_kernel, nest_rows, nest_total, nest_cols),
+        out_shape=(
+            jax.ShapeDtypeStruct(parent.shape, f32),
+            jax.ShapeDtypeStruct(nest_state.shape, f32),
         ),
+        grid=(tile_rows // ROWS,),
+        in_specs=[
+            smem, lines,
+            pl.BlockSpec(feed.shape, lambda i: (0, 0, 0, 0)),
+            pl.BlockSpec(nest_new.shape, lambda i: (0, 0, 0)),
+        ],
+        out_specs=(lines, pl.BlockSpec(nest_state.shape, lambda i: (0, 0, 0, 0))),
         compiler_params=pltpu.CompilerParams(vmem_limit_bytes=VMEM_LIMIT),
-        name="parent_step",
-    )(place, parent, parent, parent, above, below, beside, parent_mix, feed)
-    return parent_out, nest_out[None]
+        name="feedback",
+    )(nest_pos, parent_new, feed, nest_new)
 
 
 def solution(mesh):

time: 61.4 us -> 46.5 us (0.76)
  local copies, waits for them, and re-layouts: 7.3 us -> 0 us
  between operations: 7.3 us -> 0.64 us
    unnamed x11 -> x0, local copies, waits for them, and re-layouts: 3.82 us -> none
    pallas_call x1, Pallas kernels: 12 us -> 9.49 us  [shards(): pl.pallas_call(functools.partial(feedback_kernel, nest_rows, nest_total,...]
    slice x2 -> x0, local copies, waits for them, and re-layouts: 2.4 us -> none  [the longest x1 1.31 us: shards(): anchor[0] + lead_x]
    pallas_call x1, Pallas kernels: 34.1 us -> 36 us  [shards(): pl.pallas_call(functools.partial(exchange_kernel, nt, nn, lo_count), out_...]
    dynamic_slice x2 -> x0, local copies, waits for them, and re-layouts: 1.08 us -> none  [the longest x1 1.03 us: shards(): strip = lax.dynamic_slice(parent, (begin, corner, 0), (win, span, width))]
where the time goes in v2:
time: 46.5 us; the launch traced here: 46.1 us
  Pallas kernels  45.5 us (98%)
  between operations  0.64 us (1%)
    pallas_call x1, Pallas kernels, shards(): pl.pallas_call(functools.partial(exchange_kernel, nt, nn, lo_count), out_...  36 us
    pallas_call x1, Pallas kernels, shards(): pl.pallas_call(functools.partial(feedback_kernel, nest_rows, nest_total,...  9.49 us

profile of v2, /device:TPU:0, one launch (start us, length us, event | category | flops | bytes accessed | tf_op | source)
XLA Modules:
  0.0 46.1 jit_solution(389245579276965656)
XLA Ops:
  0.6 36.0 %nest_exchange.1 = (f32[4,128,128]{2,1,0:T(8,128)}, f32[8,2,48,128]{3,2,1,0:T(8,128)}, f32[64,256,128]{2,1,0:T(8,128)}) custom-call(s32[1,2]{1,0:T(1,128)} %pos.3, f32[64,256,128]{2,1,0:T(8,128)} %parent_hbm.1, f32[1,4,128,128]{3,2,1,0:T(8,128)} %state_hbm.1, f32[128,128]{1,0:T(8,128)} %pmix_hbm.1, f32[128,128]{1,0:T(8,128)} %nmix_hbm.1, f32[2,128]{1,0:T(2,128)} %courant_hbm.1), custom_call_target="tpu_custom_call" | custom-call | tf_op jit(solution)/shard_map/nest_exchange/pallas_call | solution.py:450
  36.7 9.5 %feedback.1 = (f32[64,256,128]{2,1,0:T(8,128)}, f32[1,4,128,128]{3,2,1,0:T(8,128)}) custom-call(s32[1,2]{1,0:T(1,128)} %pos.3, f32[64,256,128]{2,1,0:T(8,128)} %get-tuple-element.5.block, f32[8,2,48,128]{3,2,1,0:T(8,128)} %get-tuple-element.6.feed, f32[4,128,128]{2,1,0:T(8,128)} %get-tuple-element.7.nest), custom_call_target="tpu_custom_call" | custom-call | tf_op jit(solution)/shard_map/feedback/pallas_call | solution.py:488

commit v3 on v2

--- a/solution.py
+++ b/solution.py
@@ -12,10 +12,12 @@
 HIGH = lax.Precision.HIGHEST
 MESH = pl.DeviceIdType.MESH
 LANES = 8
-ROWS = 8
 CHUNK = 4
+GROUP = 2
+LOADS = 4
 PAD = 8
-VMEM_LIMIT = 56 * 1024 * 1024
+VMEM_LIMIT = 40 * 1024 * 1024
+FEED_LIMIT = 16 * 1024 * 1024
 
 
 def split_operator(mix):
@@ -42,10 +44,10 @@
 
 def exchange_kernel(
     nt, nn, lo_count, pos, parent_hbm, state_hbm, pmix_hbm, nmix_hbm, courant_hbm,
-    nest_out, feed, parent_new,
-    held, fresh, band, edges, above, below, beside, state, pmix, nmix, courant,
-    arrived, reduced, rows, halo, start, current,
-    load, store, send1, recv1, send2, recv2, send3, recv3, send4, recv4,
+    nest_out, feed, fresh,
+    held, band, edges, above, below, beside, state, pmix, nmix, courant,
+    arrived, reduced, rows, halo, current,
+    load, send1, recv1, send2, recv2, send3, recv3, send4, recv4,
 ):
     t = lax.axis_index("tiles")
     n = lax.axis_index("nests")
@@ -65,16 +67,21 @@
             device_id=(tile, nest), device_id_type=MESH,
         )
 
-    loads = [
+    share = tile_rows // LOADS
+    parent_loads = [
         pltpu.make_async_copy(
-            parent_hbm, held.at[pl.ds(1, tile_rows), pl.ds(PAD, tile_cols)], load.at[0]
-        ),
-        pltpu.make_async_copy(pmix_hbm, pmix, load.at[1]),
-        pltpu.make_async_copy(state_hbm.at[0], state, load.at[2]),
-        pltpu.make_async_copy(nmix_hbm, nmix, load.at[3]),
-        pltpu.make_async_copy(courant_hbm, courant, load.at[4]),
+            parent_hbm.at[pl.ds(i * share, share)],
+            held.at[pl.ds(1 + i * share, share), pl.ds(PAD, tile_cols)], load.at[i],
+        )
+        for i in range(LOADS)
     ]
-    for copy in loads:
+    small_loads = [
+        pltpu.make_async_copy(pmix_hbm, pmix, load.at[LOADS]),
+        pltpu.make_async_copy(state_hbm.at[0], state, load.at[LOADS + 1]),
+        pltpu.make_async_copy(nmix_hbm, nmix, load.at[LOADS + 2]),
+        pltpu.make_async_copy(courant_hbm, courant, load.at[LOADS + 3]),
+    ]
+    for copy in parent_loads + small_loads:
         copy.start()
 
     barrier = pltpu.get_barrier_semaphore()
@@ -141,7 +148,8 @@
     def _():
         halo_copy().start()
 
-    loads[0].wait()
+    for copy in parent_loads:
+        copy.wait()
 
     local = pos[0, 0] // 3 - t * tile_rows
     corner = jnp.clip(pos[0, 1] // 3 - n * tile_cols, 0, tile_cols - span)
@@ -173,25 +181,24 @@
     def _():
         left_copy().start()
 
-    for copy in loads[1:]:
+    for copy in small_loads:
         copy.wait()
     parent_operator = split_operator(pmix[...])
 
     def parent_rows(step, carry):
-        half = tile_cols // 2
-        for i in range(CHUNK):
+        for i in range(0, CHUNK, GROUP):
             row = step * CHUNK + i
-            for begin in (0, half):
-                at = PAD + begin
-                value = held[row + 1, at:at + half]
-                around = (
-                    held[row, at:at + half] + held[row + 2, at:at + half]
-                    + held[row + 1, at + 1:at + 1 + half] + held[row + 1, at - 1:at - 1 + half]
-                )
-                fresh[row, begin:begin + half] = (
-                    value + KAPPA * (around - 4.0 * value)
-                    + apply_operator(value, parent_operator)
-                )
+            value = held[pl.ds(row + 1, GROUP), PAD:PAD + tile_cols]
+            around = (
+                held[pl.ds(row, GROUP), PAD:PAD + tile_cols]
+                + held[pl.ds(row + 2, GROUP), PAD:PAD + tile_cols]
+                + held[pl.ds(row + 1, GROUP), PAD + 1:PAD + 1 + tile_cols]
+                + held[pl.ds(row + 1, GROUP), PAD - 1:PAD - 1 + tile_cols]
+            )
+            mixed = apply_operator(value.reshape(GROUP * tile_cols, width), parent_operator)
+            fresh[pl.ds(row, GROUP)] = (
+                value + KAPPA * (around - 4.0 * value) + mixed.reshape(value.shape)
+            )
         return carry
 
     chunks = tile_rows // CHUNK
@@ -281,23 +288,23 @@
             interp = term if interp is None else interp + term
         own = halo[k] if k < STEPS else state[k - STEPS]
         value = 0.5 * (own + interp)
-        start[k] = value
-        current[k] = value
-
+        if k == STEPS:
+            top = value
+        current[k, PAD:] = value
+        current[k, PAD - 1:PAD] = value[0:1]
+
+    current[STEPS - 1, PAD:] = jnp.where(first, top, current[STEPS - 1, PAD:])
     along_x = courant[0:1]
     along_y = courant[1:2]
-    at_edge = lax.broadcasted_iota(jnp.int32, (nest_cols, width), 0) == 0
     for step in range(STEPS):
-        for k in range(total - 1, step, -1):
-            value = current[k]
-            upper = current[k - 1]
-            if k == STEPS:
-                upper = jnp.where(first, start[k], upper)
-            left = jnp.where(at_edge, start[k, 0:1], pltpu.roll(value, 1, 0))
-            current[k] = (
-                value + along_x * (upper - value) + along_y * (left - value)
-                + apply_operator(value, operator)
-            )
+        value = current[step + 1:, PAD:]
+        upper = current[step:total - 1, PAD:]
+        left = current[step + 1:, PAD - 1:PAD - 1 + nest_cols]
+        mixed = apply_operator(value.reshape(-1, width), operator).reshape(value.shape)
+        value = value + along_x * (upper - value) + along_y * (left - value) + mixed
+        current[step + 1:, PAD:] = value
+        if step < STEPS - 1:
+            current[STEPS - 1, PAD:] = jnp.where(first, top, value[STEPS - 2 - step])
 
     lead_x = lax.rem(3 - lax.rem(shift_x + base, 3), 3)
     lead_y = lax.rem(3 - shift_y, 3)
@@ -306,7 +313,7 @@
         lax.broadcasted_iota(jnp.int32, (cells, nest_cols), 1)
         == lead_y + 3 * lax.broadcasted_iota(jnp.int32, (cells, nest_cols), 0)
     ).astype(jnp.float32)
-    r0, r1, r2, r3 = (current[STEPS + i] for i in range(nest_rows))
+    r0, r1, r2, r3 = (current[STEPS + i, PAD:] for i in range(nest_rows))
     chosen = jnp.where(lead_x == 0, r0, jnp.where(lead_x == 1, r1, r2))
     feed[t, 0] = jnp.dot(pick, chosen, precision=HIGH, preferred_element_type=jnp.float32)
     feed[t, 1] = jnp.dot(pick, r3, precision=HIGH, preferred_element_type=jnp.float32)
@@ -325,7 +332,7 @@
         sends.append(feed_copy(t, hi * lo_count + lax.rem(lo + step, lo_count), len(sends)))
         sends[-1].start()
 
-    nest_out[...] = current[STEPS:]
+    nest_out[...] = current[STEPS:, PAD:]
     lax.fori_loop(marks[2], marks[3], parent_rows, 0)
 
     for step in range(1, hi_count):
@@ -358,8 +365,6 @@
     fresh[tile_rows - 1] += KAPPA * below[...]
     fresh[:, 0] += KAPPA * beside[0]
     fresh[:, tile_cols - 1] += KAPPA * beside[1]
-    out_copy = pltpu.make_async_copy(fresh, parent_new, store.at[0])
-    out_copy.start()
 
     for across in range(1, lo_count):
         for step in range(hi_count):
@@ -393,41 +398,64 @@
     @pl.when(n > 0)
     def _():
         left_copy().wait_send()
-    out_copy.wait()
-
-
-def feedback_kernel(nest_rows, nest_total, nest_cols, pos, block, feed, nest, out, nest_out):
-    step = pl.program_id(0)
-    lines, cols, width = block.shape
-    tile_rows = lines * pl.num_programs(0)
-
-    @pl.when(step == 0)
-    def _():
-        nest_out[0] = nest[...]
-
-    out[...] = block[...]
+
+
+def feedback_kernel(
+    nest_rows, nest_total, nest_cols, pos, fresh, feed, nest, out, nest_out, patch, store, patched
+):
+    tile_rows, cols, width = fresh.shape
+    share = tile_rows // LOADS
+    copies = [
+        pltpu.make_async_copy(
+            fresh.at[pl.ds(i * share, share)], out.at[pl.ds(i * share, share)], store.at[i]
+        )
+        for i in range(LOADS)
+    ]
+    copies.append(pltpu.make_async_copy(nest, nest_out.at[0], store.at[LOADS]))
+    for copy in copies:
+        copy.start()
     lead_x = lax.rem(3 - lax.rem(pos[0, 0], 3), 3)
     lead_y = lax.rem(3 - lax.rem(pos[0, 1], 3), 3)
     top = (pos[0, 0] + lead_x) // 3 - lax.axis_index("tiles") * tile_rows
     first_col = (pos[0, 1] + lead_y) // 3 - lax.axis_index("nests") * cols
-    cells = feed.shape[2]
-    window = cells + 8
-    base_col = pl.multiple_of(first_col // 8 * 8, 8)
+    window = patch.shape[1]
+    base_col = pl.multiple_of(jnp.clip(first_col // 8 * 8, 0, cols - window), 8)
     offset = first_col - base_col
     limit = (nest_cols - lead_y + 2) // 3
-    for i in range(lines):
-        x = lead_x + 3 * (step * lines + i - top)
-
-        @pl.when((x >= 0) & (x < nest_total))
-        def _():
+    cell = lax.broadcasted_iota(jnp.int32, (window, width), 0) - offset
+    live = (cell >= 0) & (cell < limit)
+
+    def fed(k):
+        return (lead_x + 3 * k < nest_total) & (top + k >= 0) & (top + k < tile_rows)
+
+    def patch_copy(k):
+        return pltpu.make_async_copy(
+            patch.at[k], out.at[top + k, pl.ds(base_col, window)], patched.at[k]
+        )
+
+    for k in range(patch.shape[0]):
+        @pl.when(fed(k))
+        def _():
+            x = lead_x + 3 * k
             sender = x // nest_rows
             slot = (x - sender * nest_rows) // 3
-            cell = lax.broadcasted_iota(jnp.int32, (window, width), 0) - offset
-            fed = jnp.concatenate([feed[sender, slot], jnp.zeros((8, width), jnp.float32)], axis=0)
-            fed = pltpu.roll(fed, offset, 0)
-            old = out[i, pl.ds(base_col, window)]
-            new = jnp.where((cell >= 0) & (cell < limit), old + 0.5 * (fed - old), old)
-            out[i, pl.ds(base_col, window)] = new
+            values = jnp.concatenate(
+                [feed[sender, slot], jnp.zeros((8, width), jnp.float32)], axis=0
+            )
+            values = pltpu.roll(values, offset, 0)
+            old = fresh[top + k, pl.ds(base_col, window)]
+            patch[k] = jnp.where(live, old + 0.5 * (values - old), old)
+
+    for copy in copies:
+        copy.wait()
+    for k in range(patch.shape[0]):
+        @pl.when(fed(k))
+        def _():
+            patch_copy(k).start()
+    for k in range(patch.shape[0]):
+        @pl.when(fed(k))
+        def _():
+            patch_copy(k).wait()
 
 
 def shards(nt, nn, parent, nest_state, parent_mix, nest_mix, courant, nest_pos):
@@ -444,21 +472,24 @@
     slots = (nest_rows + 2) // 3
     vmem = pl.BlockSpec(memory_space=pltpu.VMEM)
     smem = pl.BlockSpec(memory_space=pltpu.SMEM)
-    hbm = pl.BlockSpec(memory_space=pl.ANY)
+    hbm = pl.BlockSpec(memory_space=pltpu.HBM)
     f32 = jnp.float32
     dma = pltpu.SemaphoreType.DMA
+    nest_pos, parent, nest_state, parent_mix, nest_mix, courant = (
+        pltpu.with_memory_space_constraint(array, pltpu.HBM)
+        for array in (nest_pos, parent, nest_state, parent_mix, nest_mix, courant)
+    )
     nest_new, feed, parent_new = pl.pallas_call(
         functools.partial(exchange_kernel, nt, nn, lo_count),
         out_shape=(
             jax.ShapeDtypeStruct((nest_rows, nest_cols, width), f32),
             jax.ShapeDtypeStruct((nt, slots, fb_cols, width), f32),
-            jax.ShapeDtypeStruct(parent.shape, f32),
+            pltpu.VMEM(parent.shape, f32),
         ),
         in_specs=[smem] + [hbm] * 5,
-        out_specs=(vmem, vmem, hbm),
+        out_specs=(vmem, vmem, vmem),
         scratch_shapes=[
             pltpu.VMEM((tile_rows + 2, tile_cols + 2 * PAD, width), f32),
-            pltpu.VMEM((tile_rows, tile_cols, width), f32),
             pltpu.VMEM((win, span, width), f32),
             pltpu.VMEM((2, tile_rows, width), f32),
             pltpu.VMEM((tile_cols, width), f32),
@@ -472,9 +503,8 @@
             pltpu.VMEM((win, LANES, width), f32),
             pltpu.VMEM((groups, count, LANES, width), f32),
             pltpu.VMEM((STEPS, nest_cols, width), f32),
-            pltpu.VMEM((nest_rows + STEPS, nest_cols, width), f32),
-            pltpu.VMEM((nest_rows + STEPS, nest_cols, width), f32),
-            dma((5,)), dma((1,)),
+            pltpu.VMEM((nest_rows + STEPS, nest_cols + PAD, width), f32),
+            dma((LOADS + 4,)),
             dma((groups,)), dma((nt,)), dma((nt,)), dma((groups,)),
             dma((5,)), dma((5,)), dma((nt - 1,)), dma((nt,)),
         ],
@@ -484,21 +514,21 @@
         name="nest_exchange",
     )(nest_pos, parent, nest_state, parent_mix, nest_mix, courant)
 
-    lines = pl.BlockSpec((ROWS, tile_cols, width), lambda i: (i, 0, 0))
+    fed_rows = (nest_total + 2) // 3
+    parent_new = pltpu.with_memory_space_constraint(parent_new, pltpu.VMEM)
     return pl.pallas_call(
         functools.partial(feedback_kernel, nest_rows, nest_total, nest_cols),
         out_shape=(
             jax.ShapeDtypeStruct(parent.shape, f32),
             jax.ShapeDtypeStruct(nest_state.shape, f32),
         ),
-        grid=(tile_rows // ROWS,),
-        in_specs=[
-            smem, lines,
-            pl.BlockSpec(feed.shape, lambda i: (0, 0, 0, 0)),
-            pl.BlockSpec(nest_new.shape, lambda i: (0, 0, 0)),
+        in_specs=[smem, vmem, vmem, vmem],
+        out_specs=(hbm, hbm),
+        scratch_shapes=[
+            pltpu.VMEM((fed_rows, fb_cols + 8, width), f32),
+            dma((LOADS + 1,)), dma((fed_rows,)),
         ],
-        out_specs=(lines, pl.BlockSpec(nest_state.shape, lambda i: (0, 0, 0, 0))),
-        compiler_params=pltpu.CompilerParams(vmem_limit_bytes=VMEM_LIMIT),
+        compiler_params=pltpu.CompilerParams(vmem_limit_bytes=FEED_LIMIT),
         name="feedback",
     )(nest_pos, parent_new, feed, nest_new)
 

time: 46.5 us -> 40.1 us (0.86)
  Pallas kernels: 45.5 us -> 39.2 us
    pallas_call x1, Pallas kernels: 9.49 us -> 4.15 us  [shards(): pl.pallas_call(functools.partial(feedback_kernel, nest_rows, nest_total,...]
    pallas_call x1, Pallas kernels: 36 us -> 35.1 us  [shards(): pl.pallas_call(functools.partial(exchange_kernel, nt, nn, lo_count), out_...]
where the time goes in v3:
time: 40.1 us; the launch traced here: 39.9 us
  Pallas kernels  39.2 us (98%)
  between operations  0.64 us (2%)
    pallas_call x1, Pallas kernels, shards(): pl.pallas_call(functools.partial(exchange_kernel, nt, nn, lo_count), out_...  35.1 us
    pallas_call x1, Pallas kernels, shards(): pl.pallas_call(functools.partial(feedback_kernel, nest_rows, nest_total,...  4.15 us

profile of v3, /device:TPU:0, one launch (start us, length us, event | category | flops | bytes accessed | tf_op | source)
XLA Modules:
  0.0 39.9 jit_solution(16702614967976860713)
XLA Ops:
  0.6 35.1 %nest_exchange.1 = (f32[4,128,128]{2,1,0:T(8,128)S(1)}, f32[8,2,48,128]{3,2,1,0:T(8,128)S(1)}, f32[64,256,128]{2,1,0:T(8,128)S(1)}) custom-call(s32[1,2]{1,0:T(1,128)} %pos.3, f32[64,256,128]{2,1,0:T(8,128)} %parent_hbm.1, f32[1,4,128,128]{3,2,1,0:T(8,128)} %state_hbm.1, f32[128,128]{1,0:T(8,128)} %pmix_hbm.1, f32[128,128]{1,0:T(8,128)} %nmix_hbm.1, ...), custom_call_target="tpu_custom_call" | custom-call | tf_op jit(solution)/shard_map/nest_exchange/pallas_call | solution.py:482
  35.7 4.2 %feedback.1 = (f32[64,256,128]{2,1,0:T(8,128)}, f32[1,4,128,128]{3,2,1,0:T(8,128)}) custom-call(s32[1,2]{1,0:T(1,128)} %pos.3, f32[64,256,128]{2,1,0:T(8,128)S(1)} %get-tuple-element.5.fresh, f32[8,2,48,128]{3,2,1,0:T(8,128)S(1)} %get-tuple-element.6.feed, f32[4,128,128]{2,1,0:T(8,128)S(1)} %get-tuple-element.7.nest), custom_call_target="tpu_custom_call" | custom-call | tf_op jit(solution)/shard_map/feedback/pallas_call | solution.py:519

commit v4 on v3

--- a/solution.py
+++ b/solution.py
@@ -55,11 +55,25 @@
     tile_rows, tile_cols, _ = fresh.shape
     win, span, _ = band.shape
     groups = span // LANES
-    count = rows.shape[1]
-    relay0 = (nt - groups) // 2
+    count = rows.shape[0]
 
     def low_row(tile):
-        return jnp.clip((tile * nest_rows - STEPS + 3) // 3 - 1, 0, win - count)
+        return (tile * nest_rows - STEPS + 3) // 3 - 1
+
+    def cut(extent, parts, index):
+        return extent * index // parts, extent * (index + 1) // parts
+
+    lows = [min(max(low_row(tile), 0), win - count) for tile in range(nt)]
+    parts = []
+    for tile in range(nt):
+        row_a, row_b = cut(win, nt // lo_count, tile // lo_count)
+        col_a, col_b = cut(groups, lo_count, tile % lo_count)
+        parts.append((row_a, row_b, col_a * LANES, col_b * LANES))
+
+    def overlap(source, target):
+        low = max(parts[source][0], lows[target])
+        high = min(parts[source][1], lows[target] + count)
+        return low, high
 
     def remote(src, dst, send, recv, tile, nest):
         return pltpu.make_async_remote_copy(
@@ -159,16 +173,18 @@
         part = held[jnp.clip(row, 0, tile_rows - 1) + 1, pl.ds(PAD + corner, span)]
         band[w] = jnp.where(inside, part, 0.0)
 
-    def gather_copy(g):
+    def gather_copy(source, target):
+        row_a, row_b, col_a, col_b = parts[target]
         return remote(
-            band.at[:, pl.ds(g * LANES, LANES)], arrived.at[t], send1.at[g], recv1.at[t],
-            relay0 + g, n,
-        )
-
-    for g in range(groups):
-        @pl.when(t != relay0 + g)
-        def _():
-            gather_copy(g).start()
+            band.at[row_a:row_b, col_a:col_b],
+            arrived.at[source, 0:row_b - row_a, 0:col_b - col_a],
+            send1.at[target], recv1.at[source], target, n,
+        )
+
+    for r in range(nt):
+        @pl.when(t != r)
+        def _():
+            gather_copy(t, r).start()
 
     edges[0] = held[1:tile_rows + 1, PAD]
     edges[1] = held[1:tile_rows + 1, PAD + tile_cols - 1]
@@ -202,42 +218,41 @@
         return carry
 
     chunks = tile_rows // CHUNK
-    marks = [0, chunks // 2, chunks * 11 // 16, chunks * 14 // 16, chunks]
+    marks = [0, chunks * 9 // 16, chunks * 12 // 16, chunks * 14 // 16, chunks]
     lax.fori_loop(marks[0], marks[1], parent_rows, 0)
 
-    is_relay = (t >= relay0) & (t < relay0 + groups)
-
-    def spread_copy(r):
+    def spread_copy(source, target):
+        row_a, _, col_a, col_b = parts[source]
+        low, high = overlap(source, target)
         return remote(
-            reduced.at[pl.ds(low_row(r), count)], rows.at[t - relay0], send2.at[r],
-            recv2.at[t - relay0], r, n,
-        )
-
-    def arrive_copy(s):
-        return remote(
-            band.at[:, pl.ds(0, LANES)], arrived.at[s], send1.at[0], recv1.at[s], s, n
-        )
-
-    for g in range(groups):
-        @pl.when(t == relay0 + g)
-        def _():
-            reduced[...] = band[:, g * LANES:(g + 1) * LANES]
-
-    for s in range(nt):
-        @pl.when(is_relay & (t != s))
-        def _():
-            arrive_copy(s).wait_recv()
-            reduced[...] += arrived[s]
+            reduced.at[low - row_a:high - row_a, 0:col_b - col_a],
+            rows.at[low - lows[target]:high - lows[target], col_a:col_b],
+            send2.at[target], recv2.at[source], target, n,
+        )
+
+    def needs(source, target):
+        low, high = overlap(source, target)
+        return low < high and parts[source][2] < parts[source][3]
 
     for r in range(nt):
-        @pl.when(is_relay & (t != r))
-        def _():
-            spread_copy(r).start()
-
-    for g in range(groups):
-        @pl.when(t == relay0 + g)
-        def _():
-            rows[g] = reduced[pl.ds(low_row(t), count)]
+        row_a, row_b, col_a, col_b = parts[r]
+
+        @pl.when(t == r)
+        def _():
+            total = band[row_a:row_b, col_a:col_b]
+            for s in range(nt):
+                if s != r:
+                    gather_copy(s, r).wait_recv()
+                    total = total + arrived[s, 0:row_b - row_a, 0:col_b - col_a]
+            reduced[0:row_b - row_a, 0:col_b - col_a] = total
+            for q in range(nt):
+                if q != r and needs(r, q):
+                    spread_copy(r, q).start()
+            low, high = overlap(r, r)
+            if needs(r, r):
+                rows[low - lows[r]:high - lows[r], col_a:col_b] = (
+                    reduced[low - row_a:high - row_a, 0:col_b - col_a]
+                )
 
     @pl.when(t < nt - 1)
     def _():
@@ -263,22 +278,22 @@
     def _():
         halo_copy().wait_recv()
 
-    for g in range(groups):
-        @pl.when(t != relay0 + g)
-        def _():
-            remote(
-                reduced.at[pl.ds(0, count)], rows.at[g], send2.at[0], recv2.at[g], t, n
-            ).wait_recv()
+    for q in range(nt):
+        @pl.when(t == q)
+        def _():
+            for r in range(nt):
+                if r != q and needs(r, q):
+                    spread_copy(r, q).wait_recv()
 
     lines = [
         jnp.dot(
-            table, rows[:, i].reshape(groups * LANES, width),
+            table, rows[i],
             precision=HIGH, preferred_element_type=jnp.float32,
         )
         for i in range(count)
     ]
     base = t * nest_rows
-    lowest = low_row(t)
+    lowest = jnp.clip(low_row(t), 0, win - count)
     total = nest_rows + STEPS
     for k in range(total):
         interp = None
@@ -373,14 +388,16 @@
 
     for copy in sends:
         copy.wait_send()
-    for g in range(groups):
-        @pl.when(t != relay0 + g)
-        def _():
-            gather_copy(g).wait_send()
     for r in range(nt):
-        @pl.when(is_relay & (t != r))
-        def _():
-            spread_copy(r).wait_send()
+        @pl.when(t != r)
+        def _():
+            gather_copy(t, r).wait_send()
+
+        @pl.when(t == r)
+        def _():
+            for q in range(nt):
+                if q != r and needs(r, q):
+                    spread_copy(r, q).wait_send()
 
     @pl.when(t < nt - 1)
     def _():
@@ -470,6 +487,8 @@
     fb_cols = -(-((nest_cols + 2) // 3) // LANES) * LANES
     lo_count = nt // 4
     slots = (nest_rows + 2) // 3
+    part_rows = -(-win // (nt // lo_count))
+    part_cols = -(-groups // lo_count) * LANES
     vmem = pl.BlockSpec(memory_space=pltpu.VMEM)
     smem = pl.BlockSpec(memory_space=pltpu.SMEM)
     hbm = pl.BlockSpec(memory_space=pltpu.HBM)
@@ -499,13 +518,13 @@
             pltpu.VMEM((width, width), f32),
             pltpu.VMEM((width, width), f32),
             pltpu.VMEM((2, width), f32),
-            pltpu.VMEM((nt, win, LANES, width), f32),
-            pltpu.VMEM((win, LANES, width), f32),
-            pltpu.VMEM((groups, count, LANES, width), f32),
+            pltpu.VMEM((nt, part_rows, part_cols, width), f32),
+            pltpu.VMEM((part_rows, part_cols, width), f32),
+            pltpu.VMEM((count, span, width), f32),
             pltpu.VMEM((STEPS, nest_cols, width), f32),
             pltpu.VMEM((nest_rows + STEPS, nest_cols + PAD, width), f32),
             dma((LOADS + 4,)),
-            dma((groups,)), dma((nt,)), dma((nt,)), dma((groups,)),
+            dma((nt,)), dma((nt,)), dma((nt,)), dma((nt,)),
             dma((5,)), dma((5,)), dma((nt - 1,)), dma((nt,)),
         ],
         compiler_params=pltpu.CompilerParams(

time: 40.1 us -> 38.1 us (0.950)
  Pallas kernels: 39.2 us -> 37.3 us
    pallas_call x1, Pallas kernels: 35.1 us -> 33.2 us  [shards(): pl.pallas_call(functools.partial(exchange_kernel, nt, nn, lo_count), out_...]
where the time goes in v4:
time: 38.1 us; the launch traced here: 38 us
  Pallas kernels  37.3 us (98%)
  between operations  0.64 us (2%)
    pallas_call x1, Pallas kernels, shards(): pl.pallas_call(functools.partial(exchange_kernel, nt, nn, lo_count), out_...  33.2 us
    pallas_call x1, Pallas kernels, shards(): pl.pallas_call(functools.partial(feedback_kernel, nest_rows, nest_total,...  4.15 us

profile of v4, /device:TPU:0, one launch (start us, length us, event | category | flops | bytes accessed | tf_op | source)
XLA Modules:
  0.0 38.0 jit_solution(8916033047326795521)
XLA Ops:
  0.6 33.2 %nest_exchange.1 = (f32[4,128,128]{2,1,0:T(8,128)S(1)}, f32[8,2,48,128]{3,2,1,0:T(8,128)S(1)}, f32[64,256,128]{2,1,0:T(8,128)S(1)}) custom-call(s32[1,2]{1,0:T(1,128)} %pos.3, f32[64,256,128]{2,1,0:T(8,128)} %parent_hbm.1, f32[1,4,128,128]{3,2,1,0:T(8,128)} %state_hbm.1, f32[128,128]{1,0:T(8,128)} %pmix_hbm.1, f32[128,128]{1,0:T(8,128)} %nmix_hbm.1, ...), custom_call_target="tpu_custom_call" | custom-call | tf_op jit(solution)/shard_map/nest_exchange/pallas_call | solution.py:501
  33.8 4.2 %feedback.1 = (f32[64,256,128]{2,1,0:T(8,128)}, f32[1,4,128,128]{3,2,1,0:T(8,128)}) custom-call(s32[1,2]{1,0:T(1,128)} %pos.3, f32[64,256,128]{2,1,0:T(8,128)S(1)} %get-tuple-element.5.fresh, f32[8,2,48,128]{3,2,1,0:T(8,128)S(1)} %get-tuple-element.6.feed, f32[4,128,128]{2,1,0:T(8,128)S(1)} %get-tuple-element.7.nest), custom_call_target="tpu_custom_call" | custom-call | tf_op jit(solution)/shard_map/feedback/pallas_call | solution.py:538

commit v5 on v4

--- a/solution.py
+++ b/solution.py
@@ -46,8 +46,8 @@
     nt, nn, lo_count, pos, parent_hbm, state_hbm, pmix_hbm, nmix_hbm, courant_hbm,
     nest_out, feed, fresh,
     held, band, edges, above, below, beside, state, pmix, nmix, courant,
-    arrived, reduced, rows, halo, current,
-    load, send1, recv1, send2, recv2, send3, recv3, send4, recv4,
+    early, mine, arrived, reduced, rows, halo, current,
+    load, send0, recv0, send1, recv1, send2, recv2, send3, recv3, send4, recv4,
 ):
     t = lax.axis_index("tiles")
     n = lax.axis_index("nests")
@@ -162,6 +162,10 @@
     def _():
         halo_copy().start()
 
+    @pl.when(t > 0)
+    def _():
+        up_copy().start()
+
     for copy in parent_loads:
         copy.wait()
 
@@ -173,18 +177,40 @@
         part = held[jnp.clip(row, 0, tile_rows - 1) + 1, pl.ds(PAD + corner, span)]
         band[w] = jnp.where(inside, part, 0.0)
 
+    hi_count = nt // lo_count
+
+    def chunk_order(tile):
+        return sorted(range(hi_count), key=lambda h: -abs(h - tile // lo_count))
+
+    def early_copy(source, target, chunk):
+        row_a, row_b, col_a, col_b = parts[chunk * lo_count + target % lo_count]
+        return remote(
+            band.at[row_a:row_b, col_a:col_b],
+            early.at[source % lo_count, row_a:row_b, 0:col_b - col_a],
+            send0.at[target % lo_count, chunk], recv0.at[source % lo_count, chunk], target, n,
+        )
+
     def gather_copy(source, target):
         row_a, row_b, col_a, col_b = parts[target]
         return remote(
-            band.at[row_a:row_b, col_a:col_b],
-            arrived.at[source, 0:row_b - row_a, 0:col_b - col_a],
-            send1.at[target], recv1.at[source], target, n,
-        )
+            mine.at[row_a:row_b, 0:col_b - col_a],
+            arrived.at[source // lo_count, 0:row_b - row_a, 0:col_b - col_a],
+            send1.at[target // lo_count], recv1.at[source // lo_count], target, n,
+        )
+
+    def same_hi(tile):
+        first_one = tile // lo_count * lo_count
+        return [other for other in range(first_one, first_one + lo_count) if other != tile]
+
+    def same_lo(tile):
+        return [other for other in range(tile % lo_count, nt, lo_count) if other != tile]
 
     for r in range(nt):
-        @pl.when(t != r)
-        def _():
-            gather_copy(t, r).start()
+        @pl.when(t == r)
+        def _():
+            for chunk in chunk_order(r):
+                for other in same_hi(r):
+                    early_copy(r, other, chunk).start()
 
     edges[0] = held[1:tile_rows + 1, PAD]
     edges[1] = held[1:tile_rows + 1, PAD + tile_cols - 1]
@@ -218,8 +244,23 @@
         return carry
 
     chunks = tile_rows // CHUNK
-    marks = [0, chunks * 9 // 16, chunks * 12 // 16, chunks * 14 // 16, chunks]
+    marks = [chunks * m // 16 for m in (0, 2, 9, 12, 14, 16)]
     lax.fori_loop(marks[0], marks[1], parent_rows, 0)
+
+    for r in range(nt):
+        @pl.when(t == r)
+        def _():
+            for chunk in chunk_order(r):
+                row_a, row_b, col_a, col_b = parts[chunk * lo_count + r % lo_count]
+                total = band[row_a:row_b, col_a:col_b]
+                for other in same_hi(r):
+                    early_copy(other, r, chunk).wait_recv()
+                    total = total + early[other % lo_count, row_a:row_b, 0:col_b - col_a]
+                mine[row_a:row_b, 0:col_b - col_a] = total
+                if chunk != r // lo_count:
+                    gather_copy(r, chunk * lo_count + r % lo_count).start()
+
+    lax.fori_loop(marks[1], marks[2], parent_rows, 0)
 
     def spread_copy(source, target):
         row_a, _, col_a, col_b = parts[source]
@@ -239,11 +280,10 @@
 
         @pl.when(t == r)
         def _():
-            total = band[row_a:row_b, col_a:col_b]
-            for s in range(nt):
-                if s != r:
-                    gather_copy(s, r).wait_recv()
-                    total = total + arrived[s, 0:row_b - row_a, 0:col_b - col_a]
+            total = mine[row_a:row_b, 0:col_b - col_a]
+            for s in same_lo(r):
+                gather_copy(s, r).wait_recv()
+                total = total + arrived[s // lo_count, 0:row_b - row_a, 0:col_b - col_a]
             reduced[0:row_b - row_a, 0:col_b - col_a] = total
             for q in range(nt):
                 if q != r and needs(r, q):
@@ -258,11 +298,7 @@
     def _():
         down_copy().start()
 
-    @pl.when(t > 0)
-    def _():
-        up_copy().start()
-
-    lax.fori_loop(marks[1], marks[2], parent_rows, 0)
+    lax.fori_loop(marks[2], marks[3], parent_rows, 0)
 
     operator = split_operator(nmix[...])
     shift_x = lax.rem(pos[0, 0], 3)
@@ -333,7 +369,6 @@
     feed[t, 0] = jnp.dot(pick, chosen, precision=HIGH, preferred_element_type=jnp.float32)
     feed[t, 1] = jnp.dot(pick, r3, precision=HIGH, preferred_element_type=jnp.float32)
 
-    hi_count = nt // lo_count
     hi, lo = t // lo_count, lax.rem(t, lo_count)
 
     def feed_copy(source, target, slot):
@@ -348,7 +383,7 @@
         sends[-1].start()
 
     nest_out[...] = current[STEPS:, PAD:]
-    lax.fori_loop(marks[2], marks[3], parent_rows, 0)
+    lax.fori_loop(marks[3], marks[4], parent_rows, 0)
 
     for step in range(1, hi_count):
         source = lax.rem(hi + step, hi_count) * lo_count + lo
@@ -358,7 +393,7 @@
             sends.append(feed_copy(source, target, len(sends)))
             sends[-1].start()
 
-    lax.fori_loop(marks[3], marks[4], parent_rows, 0)
+    lax.fori_loop(marks[4], marks[5], parent_rows, 0)
 
     @pl.when(t > 0)
     def _():
@@ -389,15 +424,16 @@
     for copy in sends:
         copy.wait_send()
     for r in range(nt):
-        @pl.when(t != r)
-        def _():
-            gather_copy(t, r).wait_send()
-
         @pl.when(t == r)
         def _():
             for q in range(nt):
                 if q != r and needs(r, q):
                     spread_copy(r, q).wait_send()
+            for other in same_lo(r):
+                gather_copy(r, other).wait_send()
+            for other in same_hi(r):
+                for chunk in range(hi_count):
+                    early_copy(r, other, chunk).wait_send()
 
     @pl.when(t < nt - 1)
     def _():
@@ -487,7 +523,8 @@
     fb_cols = -(-((nest_cols + 2) // 3) // LANES) * LANES
     lo_count = nt // 4
     slots = (nest_rows + 2) // 3
-    part_rows = -(-win // (nt // lo_count))
+    hi_count = nt // lo_count
+    part_rows = -(-win // hi_count)
     part_cols = -(-groups // lo_count) * LANES
     vmem = pl.BlockSpec(memory_space=pltpu.VMEM)
     smem = pl.BlockSpec(memory_space=pltpu.SMEM)
@@ -518,13 +555,16 @@
             pltpu.VMEM((width, width), f32),
             pltpu.VMEM((width, width), f32),
             pltpu.VMEM((2, width), f32),
-            pltpu.VMEM((nt, part_rows, part_cols, width), f32),
+            pltpu.VMEM((lo_count, win, part_cols, width), f32),
+            pltpu.VMEM((win, part_cols, width), f32),
+            pltpu.VMEM((hi_count, part_rows, part_cols, width), f32),
             pltpu.VMEM((part_rows, part_cols, width), f32),
             pltpu.VMEM((count, span, width), f32),
             pltpu.VMEM((STEPS, nest_cols, width), f32),
             pltpu.VMEM((nest_rows + STEPS, nest_cols + PAD, width), f32),
             dma((LOADS + 4,)),
-            dma((nt,)), dma((nt,)), dma((nt,)), dma((nt,)),
+            dma((lo_count, hi_count)), dma((lo_count, hi_count)),
+            dma((hi_count,)), dma((hi_count,)), dma((nt,)), dma((nt,)),
             dma((5,)), dma((5,)), dma((nt - 1,)), dma((nt,)),
         ],
         compiler_params=pltpu.CompilerParams(

time: 38.1 us -> 41.3 us (1.084)
  Pallas kernels: 37.3 us -> 40.5 us
    pallas_call x1, Pallas kernels: 33.2 us -> 36.3 us  [shards(): pl.pallas_call(functools.partial(exchange_kernel, nt, nn, lo_count), out_...]
where the time goes in v5:
time: 41.3 us; the launch traced here: 41.1 us
  Pallas kernels  40.5 us (98%)
  between operations  0.64 us (2%)
    pallas_call x1, Pallas kernels, shards(): pl.pallas_call(functools.partial(exchange_kernel, nt, nn, lo_count), out_...  36.3 us
    pallas_call x1, Pallas kernels, shards(): pl.pallas_call(functools.partial(feedback_kernel, nest_rows, nest_total,...  4.15 us

profile of v5, /device:TPU:0, one launch (start us, length us, event | category | flops | bytes accessed | tf_op | source)
XLA Modules:
  0.0 41.1 jit_solution(8004484667652132064)
XLA Ops:
  0.6 36.3 %nest_exchange.1 = (f32[4,128,128]{2,1,0:T(8,128)S(1)}, f32[8,2,48,128]{3,2,1,0:T(8,128)S(1)}, f32[64,256,128]{2,1,0:T(8,128)S(1)}) custom-call(s32[1,2]{1,0:T(1,128)} %pos.3, f32[64,256,128]{2,1,0:T(8,128)} %parent_hbm.1, f32[1,4,128,128]{3,2,1,0:T(8,128)} %state_hbm.1, f32[128,128]{1,0:T(8,128)} %pmix_hbm.1, f32[128,128]{1,0:T(8,128)} %nmix_hbm.1, ...), custom_call_target="tpu_custom_call" | custom-call | tf_op jit(solution)/shard_map/nest_exchange/pallas_call | solution.py:538
  37.0 4.2 %feedback.1 = (f32[64,256,128]{2,1,0:T(8,128)}, f32[1,4,128,128]{3,2,1,0:T(8,128)}) custom-call(s32[1,2]{1,0:T(1,128)} %pos.3, f32[64,256,128]{2,1,0:T(8,128)S(1)} %get-tuple-element.5.fresh, f32[8,2,48,128]{3,2,1,0:T(8,128)S(1)} %get-tuple-element.6.feed, f32[4,128,128]{2,1,0:T(8,128)S(1)} %get-tuple-element.7.nest), custom_call_target="tpu_custom_call" | custom-call | tf_op jit(solution)/shard_map/feedback/pallas_call | solution.py:578

commit v6 on v4

--- a/solution.py
+++ b/solution.py
@@ -9,7 +9,6 @@
 
 STEPS = 3
 KAPPA = 0.125
-HIGH = lax.Precision.HIGHEST
 MESH = pl.DeviceIdType.MESH
 LANES = 8
 CHUNK = 4
@@ -39,7 +38,18 @@
 
 
 def hat(distance):
-    return jnp.maximum(3 - jnp.abs(distance), 0).astype(jnp.float32) * (1.0 / 3.0)
+    return jnp.maximum(3 - jnp.abs(distance), 0).astype(jnp.float32)
+
+
+def apply_table(table, values):
+    width = values.shape[-1]
+    high = values.astype(jnp.bfloat16)
+    low = (values - high.astype(jnp.float32)).astype(jnp.bfloat16)
+    both = jnp.dot(
+        table.astype(jnp.bfloat16), jnp.concatenate([high, low], axis=1),
+        preferred_element_type=jnp.float32,
+    )
+    return both[:, :width] + both[:, width:]
 
 
 def exchange_kernel(
@@ -66,7 +76,7 @@
     lows = [min(max(low_row(tile), 0), win - count) for tile in range(nt)]
     parts = []
     for tile in range(nt):
-        row_a, row_b = cut(win, nt // lo_count, tile // lo_count)
+        row_a, row_b = (-(-win * i // (nt // lo_count)) for i in (tile // lo_count, tile // lo_count + 1))
         col_a, col_b = cut(groups, lo_count, tile % lo_count)
         parts.append((row_a, row_b, col_a * LANES, col_b * LANES))
 
@@ -161,6 +171,10 @@
     @pl.when(t < nt - 1)
     def _():
         halo_copy().start()
+
+    @pl.when(t > 0)
+    def _():
+        up_copy().start()
 
     for copy in parent_loads:
         copy.wait()
@@ -254,14 +268,6 @@
                     reduced[low - row_a:high - row_a, 0:col_b - col_a]
                 )
 
-    @pl.when(t < nt - 1)
-    def _():
-        down_copy().start()
-
-    @pl.when(t > 0)
-    def _():
-        up_copy().start()
-
     lax.fori_loop(marks[1], marks[2], parent_rows, 0)
 
     operator = split_operator(nmix[...])
@@ -285,13 +291,7 @@
                 if r != q and needs(r, q):
                     spread_copy(r, q).wait_recv()
 
-    lines = [
-        jnp.dot(
-            table, rows[i],
-            precision=HIGH, preferred_element_type=jnp.float32,
-        )
-        for i in range(count)
-    ]
+    lines = [apply_table(table, rows[i]) * (1.0 / 9.0) for i in range(count)]
     base = t * nest_rows
     lowest = jnp.clip(low_row(t), 0, win - count)
     total = nest_rows + STEPS
@@ -330,8 +330,8 @@
     ).astype(jnp.float32)
     r0, r1, r2, r3 = (current[STEPS + i, PAD:] for i in range(nest_rows))
     chosen = jnp.where(lead_x == 0, r0, jnp.where(lead_x == 1, r1, r2))
-    feed[t, 0] = jnp.dot(pick, chosen, precision=HIGH, preferred_element_type=jnp.float32)
-    feed[t, 1] = jnp.dot(pick, r3, precision=HIGH, preferred_element_type=jnp.float32)
+    feed[t, 0] = apply_table(pick, chosen)
+    feed[t, 1] = apply_table(pick, r3)
 
     hi_count = nt // lo_count
     hi, lo = t // lo_count, lax.rem(t, lo_count)
@@ -346,6 +346,10 @@
     for step in range(1, lo_count):
         sends.append(feed_copy(t, hi * lo_count + lax.rem(lo + step, lo_count), len(sends)))
         sends[-1].start()
+
+    @pl.when(t < nt - 1)
+    def _():
+        down_copy().start()
 
     nest_out[...] = current[STEPS:, PAD:]
     lax.fori_loop(marks[2], marks[3], parent_rows, 0)

time: 38.1 us -> 37.1 us (0.974)
  Pallas kernels: 37.3 us -> 36.3 us
    pallas_call x1, Pallas kernels: 33.2 us -> 32.1 us  [shards(): pl.pallas_call(functools.partial(exchange_kernel, nt, nn, lo_count), out_...]
where the time goes in v6:
time: 37.1 us; the launch traced here: 36.9 us
  Pallas kernels  36.3 us (98%)
  between operations  0.64 us (2%)
    pallas_call x1, Pallas kernels, shards(): pl.pallas_call(functools.partial(exchange_kernel, nt, nn, lo_count), out_...  32.1 us
    pallas_call x1, Pallas kernels, shards(): pl.pallas_call(functools.partial(feedback_kernel, nest_rows, nest_total,...  4.15 us

profile of v6, /device:TPU:0, one launch (start us, length us, event | category | flops | bytes accessed | tf_op | source)
XLA Modules:
  0.0 36.9 jit_solution(12939504012003481835)
XLA Ops:
  0.6 32.1 %nest_exchange.1 = (f32[4,128,128]{2,1,0:T(8,128)S(1)}, f32[8,2,48,128]{3,2,1,0:T(8,128)S(1)}, f32[64,256,128]{2,1,0:T(8,128)S(1)}) custom-call(s32[1,2]{1,0:T(1,128)} %pos.3, f32[64,256,128]{2,1,0:T(8,128)} %parent_hbm.1, f32[1,4,128,128]{3,2,1,0:T(8,128)} %state_hbm.1, f32[128,128]{1,0:T(8,128)} %pmix_hbm.1, f32[128,128]{1,0:T(8,128)} %nmix_hbm.1, ...), custom_call_target="tpu_custom_call" | custom-call | tf_op jit(solution)/shard_map/nest_exchange/pallas_call | solution.py:505
  32.8 4.2 %feedback.1 = (f32[64,256,128]{2,1,0:T(8,128)}, f32[1,4,128,128]{3,2,1,0:T(8,128)}) custom-call(s32[1,2]{1,0:T(1,128)} %pos.3, f32[64,256,128]{2,1,0:T(8,128)S(1)} %get-tuple-element.5.fresh, f32[8,2,48,128]{3,2,1,0:T(8,128)S(1)} %get-tuple-element.6.feed, f32[4,128,128]{2,1,0:T(8,128)S(1)} %get-tuple-element.7.nest), custom_call_target="tpu_custom_call" | custom-call | tf_op jit(solution)/shard_map/feedback/pallas_call | solution.py:542

commit v7 on v6

--- a/solution.py
+++ b/solution.py
@@ -267,6 +267,10 @@
                 rows[low - lows[r]:high - lows[r], col_a:col_b] = (
                     reduced[low - row_a:high - row_a, 0:col_b - col_a]
                 )
+
+    @pl.when(t < nt - 1)
+    def _():
+        down_copy().start()
 
     lax.fori_loop(marks[1], marks[2], parent_rows, 0)
 
@@ -346,10 +350,6 @@
     for step in range(1, lo_count):
         sends.append(feed_copy(t, hi * lo_count + lax.rem(lo + step, lo_count), len(sends)))
         sends[-1].start()
-
-    @pl.when(t < nt - 1)
-    def _():
-        down_copy().start()
 
     nest_out[...] = current[STEPS:, PAD:]
     lax.fori_loop(marks[2], marks[3], parent_rows, 0)

time: 37.1 us -> 37.3 us (level)
  no operation moved by 1% of the time
where the time goes in v7:
time: 37.3 us; the launch traced here: 37.1 us
  Pallas kernels  36.4 us (98%)
  between operations  0.64 us (2%)
    pallas_call x1, Pallas kernels, shards(): pl.pallas_call(functools.partial(exchange_kernel, nt, nn, lo_count), out_...  32.3 us
    pallas_call x1, Pallas kernels, shards(): pl.pallas_call(functools.partial(feedback_kernel, nest_rows, nest_total,...  4.15 us

profile of v7, /device:TPU:0, one launch (start us, length us, event | category | flops | bytes accessed | tf_op | source)
XLA Modules:
  0.0 37.1 jit_solution(3771689931747603871)
XLA Ops:
  0.6 32.3 %nest_exchange.1 = (f32[4,128,128]{2,1,0:T(8,128)S(1)}, f32[8,2,48,128]{3,2,1,0:T(8,128)S(1)}, f32[64,256,128]{2,1,0:T(8,128)S(1)}) custom-call(s32[1,2]{1,0:T(1,128)} %pos.3, f32[64,256,128]{2,1,0:T(8,128)} %parent_hbm.1, f32[1,4,128,128]{3,2,1,0:T(8,128)} %state_hbm.1, f32[128,128]{1,0:T(8,128)} %pmix_hbm.1, f32[128,128]{1,0:T(8,128)} %nmix_hbm.1, ...), custom_call_target="tpu_custom_call" | custom-call | tf_op jit(solution)/shard_map/nest_exchange/pallas_call | solution.py:505
  32.9 4.2 %feedback.1 = (f32[64,256,128]{2,1,0:T(8,128)}, f32[1,4,128,128]{3,2,1,0:T(8,128)}) custom-call(s32[1,2]{1,0:T(1,128)} %pos.3, f32[64,256,128]{2,1,0:T(8,128)S(1)} %get-tuple-element.5.fresh, f32[8,2,48,128]{3,2,1,0:T(8,128)S(1)} %get-tuple-element.6.feed, f32[4,128,128]{2,1,0:T(8,128)S(1)} %get-tuple-element.7.nest), custom_call_target="tpu_custom_call" | custom-call | tf_op jit(solution)/shard_map/feedback/pallas_call | solution.py:542
